TPU v7x, 256 devices: a whole 4x4x8 slice. The times are simulated.
256 devices in a mesh: seq: 64 (over y_hi, x, z), head: 4 (over y_lo, core).
Axes of the slice: x: 4, y: 4 (y_hi: 2, y_lo: 2; y = y_hi * 2 + y_lo), z: 8, core: 2. Of those that a mesh axis runs over, the one named last changes fastest.
Arguments:
- query_in: bfloat16 [8192, 1024], P('seq', 'head'), may hold values from -180 to 180
- key_in: bfloat16 [8192, 1024], P('seq', 'head'), may hold values from -4.6 to 4.6
- value_in: bfloat16 [8192, 1024], P('seq', 'head'), may hold values from -6 to 6
- grad_out: bfloat16 [8192, 1024], P('seq', 'head'), may hold values from -6 to 6
- embedding: bfloat16 [8192, 64], P('seq'), may hold values from -1.1953125 to 1.1953125
- bias_gain: float32 [16], P('head'), may hold values from 0.5 to 2
Outputs:
- grad_query: bfloat16 [8192, 1024], P('seq', 'head')
- grad_key: bfloat16 [8192, 1024], P('seq', 'head')
- grad_value: bfloat16 [8192, 1024], P('seq', 'head')
- grad_embedding: float32 [8192, 64], P('seq')
All inputs are finite; a program needn't handle non-finite values.
Results may differ from a plain program's by a relative error of at most 0.013.
Values may be sent and summed in bfloat16 or wider, within the bound.
A program may use at most 64 MiB of HBM per device.

v0:
```python
import jax
import jax.numpy as jnp
from jax import lax
from jax.sharding import PartitionSpec as P

block_rows = 1024


def distances(left, right):
    cross = jnp.dot(
        left, right.T, precision=lax.Precision.HIGHEST, preferred_element_type=jnp.float32
    )
    left_sq = jnp.sum(left * left, axis=1)
    right_sq = jnp.sum(right * right, axis=1)
    return left_sq[:, None] + right_sq[None, :] - 2.0 * cross


def score_block(row_heads, col_heads, row_emb, col_emb, bias_gain, scaling):
    products = jnp.einsum("qhd,khd->hqk", row_heads, col_heads, preferred_element_type=jnp.float32)
    return products * scaling - bias_gain[:, None, None] * distances(row_emb, col_emb)[None]


def over_blocks(update, carried, pieces):
    total_rows = pieces[0].shape[0]

    def advance(block_num, carried_now):
        offset = block_num * block_rows
        pieces_now = tuple(
            (lax.dynamic_slice_in_dim(piece, offset, block_rows, 0) for piece in pieces)
        )
        return update(carried_now, pieces_now, offset)

    return lax.fori_loop(0, total_rows // block_rows, advance, carried)


def on_device(query_in, key_in, value_in, grad_out, embedding, bias_gain):
    row_count = query_in.shape[0]
    heads_here = bias_gain.shape[0]
    head_size = query_in.shape[1] // heads_here
    scaling = head_size ** (-0.5)
    own_q = query_in.reshape(row_count, heads_here, head_size)
    own_k = key_in.reshape(row_count, heads_here, head_size)
    own_v = value_in.reshape(row_count, heads_here, head_size)
    own_grad = grad_out.reshape(row_count, heads_here, head_size)
    own_emb = embedding.astype(jnp.float32)
    emb_count = embedding.shape[1]
    forward_init = (
        jnp.full((heads_here, row_count), -jnp.inf, jnp.float32),
        jnp.zeros((heads_here, row_count), jnp.float32),
        jnp.zeros((heads_here, row_count, head_size), jnp.float32),
    )
    query_init = (
        jnp.zeros((row_count, heads_here, head_size), jnp.float32),
        jnp.zeros((row_count,), jnp.float32),
        jnp.zeros((row_count, emb_count), jnp.float32),
    )

    def update(carried_now, pieces_now, offset):
        run_max, run_sum, weighted = carried_now
        key_blk, val_blk, emb_blk = pieces_now
        blk_len = key_blk.shape[0]
        key_heads = key_blk.reshape(blk_len, heads_here, head_size)
        val_heads = val_blk.reshape(blk_len, heads_here, head_size)
        scores = score_block(
            own_q, key_heads, own_emb, emb_blk.astype(jnp.float32), bias_gain, scaling
        )
        new_max = jnp.maximum(run_max, jnp.max(scores, axis=2))
        shrink = jnp.exp(run_max - new_max)
        weights = jnp.exp(scores - new_max[:, :, None])
        run_sum = run_sum * shrink + jnp.sum(weights, axis=2)
        weighted = weighted * shrink[:, :, None] + jnp.einsum(
            "hqk,khd->hqd", weights, val_heads.astype(jnp.float32), precision=lax.Precision.HIGHEST
        )
        return (new_max, run_sum, weighted)

    run_max, run_sum, weighted = over_blocks(
        update,
        forward_init,
        (
            lax.all_gather(key_in, "seq", axis=0, tiled=True),
            lax.all_gather(value_in, "seq", axis=0, tiled=True),
            lax.all_gather(embedding, "seq", axis=0, tiled=True),
        ),
    )
    log_total = run_max + jnp.log(run_sum)
    attended = weighted / run_sum[:, :, None]
    row_delta = jnp.einsum(
        "qhd,hqd->hq", own_grad.astype(jnp.float32), attended, precision=lax.Precision.HIGHEST
    )

    def update(carried_now, pieces_now, offset):
        grad_rows, row_total, pulled = carried_now
        key_blk, val_blk, emb_blk = pieces_now
        blk_len = key_blk.shape[0]
        key_heads = key_blk.reshape(blk_len, heads_here, head_size)
        val_heads = val_blk.reshape(blk_len, heads_here, head_size)
        emb_float = emb_blk.astype(jnp.float32)
        scores = score_block(own_q, key_heads, own_emb, emb_float, bias_gain, scaling)
        weights = jnp.exp(scores - log_total[:, :, None])
        grad_prob = jnp.einsum(
            "qhd,khd->hqk", own_grad, val_heads, preferred_element_type=jnp.float32
        )
        grad_score = weights * (grad_prob - row_delta[:, :, None])
        grad_rows = grad_rows + jnp.einsum(
            "hqk,khd->qhd",
            grad_score.astype(jnp.bfloat16),
            key_heads,
            preferred_element_type=jnp.float32,
        )
        grad_bias = -jnp.einsum("h,hqk->qk", bias_gain, grad_score, precision=lax.Precision.HIGHEST)
        row_total = row_total + jnp.sum(grad_bias, axis=1)
        pulled = pulled + jnp.dot(grad_bias, emb_float, precision=lax.Precision.HIGHEST)
        return (grad_rows, row_total, pulled)

    grad_rows, row_total, pulled = over_blocks(
        update,
        query_init,
        (
            lax.all_gather(key_in, "seq", axis=0, tiled=True),
            lax.all_gather(value_in, "seq", axis=0, tiled=True),
            lax.all_gather(embedding, "seq", axis=0, tiled=True),
        ),
    )
    query_side = 2.0 * (row_total[:, None] * own_emb - pulled)
    all_log, all_delta = (
        lax.all_gather(log_total.T, "seq", axis=0, tiled=True),
        lax.all_gather(row_delta.T, "seq", axis=0, tiled=True),
    )
    key_init = (
        jnp.zeros((row_count, heads_here, head_size), jnp.float32),
        jnp.zeros((row_count, heads_here, head_size), jnp.float32),
        jnp.zeros((row_count,), jnp.float32),
        jnp.zeros((row_count, emb_count), jnp.float32),
    )

    def update(carried_now, pieces_now, offset):
        grad_keys, grad_vals, col_total, pushed = carried_now
        query_blk, grad_blk, emb_blk = pieces_now
        blk_len = query_blk.shape[0]
        query_heads = query_blk.reshape(blk_len, heads_here, head_size)
        grad_heads = grad_blk.reshape(blk_len, heads_here, head_size)
        emb_float = emb_blk.astype(jnp.float32)
        log_blk = lax.dynamic_slice_in_dim(all_log, offset, blk_len, 0)
        delta_blk = lax.dynamic_slice_in_dim(all_delta, offset, blk_len, 0)
        scores = score_block(query_heads, own_k, emb_float, own_emb, bias_gain, scaling)
        weights = jnp.exp(scores - log_blk.T[:, :, None])
        grad_prob = jnp.einsum(
            "qhd,khd->hqk", grad_heads, own_v, preferred_element_type=jnp.float32
        )
        grad_score = weights * (grad_prob - delta_blk.T[:, :, None])
        grad_keys = grad_keys + jnp.einsum(
            "hqk,qhd->khd",
            grad_score.astype(jnp.bfloat16),
            query_heads,
            preferred_element_type=jnp.float32,
        )
        grad_vals = grad_vals + jnp.einsum(
            "hqk,qhd->khd",
            weights.astype(jnp.bfloat16),
            grad_heads,
            preferred_element_type=jnp.float32,
        )
        grad_bias = -jnp.einsum("h,hqk->qk", bias_gain, grad_score, precision=lax.Precision.HIGHEST)
        col_total = col_total + jnp.sum(grad_bias, axis=0)
        pushed = pushed + jnp.dot(grad_bias.T, emb_float, precision=lax.Precision.HIGHEST)
        return (grad_keys, grad_vals, col_total, pushed)

    grad_keys, grad_vals, col_total, pushed = over_blocks(
        update,
        key_init,
        (
            lax.all_gather(query_in, "seq", axis=0, tiled=True),
            lax.all_gather(grad_out, "seq", axis=0, tiled=True),
            lax.all_gather(embedding, "seq", axis=0, tiled=True),
        ),
    )
    key_side = 2.0 * (col_total[:, None] * own_emb - pushed)
    grad_embedding = lax.psum((query_side + key_side).astype(jnp.bfloat16), "head").astype(
        jnp.float32
    )
    grad_query = (
        (grad_rows * scaling).astype(jnp.bfloat16).reshape(row_count, heads_here * head_size)
    )
    grad_key = (grad_keys * scaling).astype(jnp.bfloat16).reshape(row_count, heads_here * head_size)
    grad_value = grad_vals.astype(jnp.bfloat16).reshape(row_count, heads_here * head_size)
    return (grad_query, grad_key, grad_value, grad_embedding)


def solution(mesh):
    placed = (
        P("seq", "head"),
        P("seq", "head"),
        P("seq", "head"),
        P("seq", "head"),
        P("seq", None),
        P("head"),
    )
    return jax.shard_map(
        on_device,
        mesh=mesh,
        in_specs=placed,
        out_specs=(P("seq", "head"), P("seq", "head"), P("seq", "head"), P("seq", None)),
        check_vma=False,
    )
```

profile of v0, /device:TPU:1, one launch (start us, length us, event | category | flops | bytes accessed | tf_op | source)
XLA Modules:
  0.0 1058.2 jit_solution(7393955058726015855)
XLA Ops:
  16.9 113.4 %all-gather.8.cloned.1.call-done = bf16[8192,64]{1,0:T(8,128)(2,1)} async-done(((bf16[128,64]{1,0:T(8,128)(2,1)}), bf16[8192,64]{1,0:T(8,128)(2,1)}) %all-gather.8.cloned.1.call-update) | async-done | bytes 1048592 | tf_op jit(solution)/shard_map/all_gather | solution.py:121
  130.3 110.4 %all-gather.6.cloned.1.call-done = bf16[8192,256]{0,1:T(8,128)(2,1)} async-done(((bf16[128,256]{0,1:T(8,128)(2,1)}), bf16[8192,256]{0,1:T(8,128)(2,1)}) %all-gather.6.cloned.1.call-update) | async-done | bytes 4194320 | tf_op jit(solution)/shard_map/all_gather | solution.py:119
  240.7 113.0 %all-gather.10.cloned.1.call-done = bf16[8192,256]{0,1:T(8,128)(2,1)} async-done(((bf16[128,256]{0,1:T(8,128)(2,1)}), bf16[8192,256]{0,1:T(8,128)(2,1)}) %all-gather.10.cloned.1.call-update) | async-done | bytes 4194320 | tf_op jit(solution)/shard_map/all_gather | solution.py:120
  353.7 48.0 %while.62 = (s32[]{:T(128)}, f32[4,128]{1,0:T(4,128)S(1)}, f32[4,128]{1,0:T(4,128)S(1)}, f32[4,128,64]{1,2,0:T(8,128)S(1)}, bf16[8192,256]{0,1:T(8,128)(2,1)}, /...) while((s32[]{:T(128)}, f32[4,128]{1,0:T(4,128)S(1)}, ...), condition=%wide.region_5.0_spmd.clone, body=%wide.region_1.5_spmd.clone.sunk | while | flops 574785024 | bytes 11543395 | solution.py:33
  401.8 117.2 %while.63 = (s32[]{:T(128)}, f32[128,4,64]{0,2,1:T(8,128)S(1)}, f32[128]{0:T(128)S(1)}, f32[128,64]{0,1:T(8,128)S(1)}, bf16[8192,256]{0,1:T(8,128)(2,1)}, /*inde...) while((s32[]{:T(128)}, f32[128,4,64]{0,2,1:T(8,128)S(1)}, ...), condition=%wide.region_9.10_spmd.clone, body=%wide.region_6.9_spmd.clone.sunk | while | flops 413547776 | bytes 22395788 | solution.py:33
  409.5 5.3 fusion.126
  438.8 5.3 fusion.126
  453.4 5.3 fusion.126
  468.1 5.3 fusion.126
  482.8 5.3 fusion.126
  497.4 5.3 fusion.126
  512.0 5.3 fusion.126
  519.7 153.2 %all_gather.29 = f32[8192,4]{0,1:T(4,128)S(1)} all-gather(f32[128,4]{0,1:T(4,128)S(1)} %bitcast.178), channel_id=1, replica_groups=mesh['seq'=64,'head'=4] {'seq'}, dimensions={0}, use_global_device_ids=true | all-gather | bytes 133120 | tf_op jit(solution)/shard_map/all_gather | solution.py:126
  672.9 147.0 %all_gather.31 = f32[8192,4]{0,1:T(4,128)S(1)} all-gather(f32[128,4]{0,1:T(4,128)S(1)} %bitcast.177), channel_id=1, replica_groups=mesh['seq'=64,'head'=4] {'seq'}, dimensions={0}, use_global_device_ids=true | all-gather | bytes 133120 | tf_op jit(solution)/shard_map/all_gather | solution.py:127
  819.9 159.3 %while.64 = (s32[]{:T(128)}, f32[128,4,64]{0,2,1:T(8,128)S(1)}, f32[128,4,64]{0,2,1:T(8,128)S(1)}, f32[128]{0:T(128)S(1)}, f32[128,64]{0,1:T(8,128)}, /*index=5*...) while((s32[]{:T(128)}, f32[128,4,64]{0,2,1:T(8,128)S(1)}, ...), condition=%wide.region_13.14_spmd.clone, body=%wide.region_10.13_spmd.clone.sunk | while | flops 481246464 | bytes 31927400 | solution.py:33
  830.4 7.3 fusion.145
  850.3 7.3 fusion.145
  870.2 7.3 fusion.145
  890.1 7.3 fusion.145
  910.0 7.3 fusion.145
  929.9 7.3 fusion.145
  949.9 7.3 fusion.145
  969.8 7.3 fusion.145
  981.6 69.5 %psum.7 = bf16[128,64]{0,1:T(8,128)(2,1)S(1)} all-reduce(bf16[128,64]{0,1:T(8,128)(2,1)S(1)} %multiply_convert_fusion.2), channel_id=1, replica_groups=mesh['seq'=64,'head'=4] {'head'}, use_global_device_ids=true, to_apply=%region_14.15 | all-reduce | flops 8192 | bytes 32768 | tf_op jit(solution)/shard_map/psum | solution.py:178
  (494 shorter events, 239.2 us)
Async XLA Ops:
  7.2 123.2 %all-gather.8.cloned.1.call-start = ((), (), s32[]{:S(2)}) async-start(), calls=%async_computation.1 | async-start | bytes 2129920 | tf_op jit(solution)/shard_map/all_gather | solution.py:121
  8.7 232.0 %all-gather.6.cloned.1.call-start = ((), (), s32[]{:S(2)}) async-start(), calls=%async_computation | async-start | bytes 4259840 | tf_op jit(solution)/shard_map/all_gather | solution.py:119
  10.3 343.3 %all-gather.10.cloned.1.call-start = ((), (), s32[]{:S(2)}) async-start(), calls=%async_computation.2 | async-start | bytes 4259840 | tf_op jit(solution)/shard_map/all_gather | solution.py:120
  12.0 807.9 %all-gather.12.cloned.1.call-start = ((), (), s32[]{:S(2)}) async-start(), calls=%async_computation.3 | async-start | bytes 4259840 | tf_op jit(solution)/shard_map/all_gather | solution.py:172
  13.6 806.3 %all-gather.14.cloned.1.call-start = ((), (), s32[]{:S(2)}) async-start(), calls=%async_computation.4 | async-start | bytes 4259840 | tf_op jit(solution)/shard_map/all_gather | solution.py:173
  353.7 48.1 %copy-start.3 = (bf16[128,256]{0,1:T(8,128)(2,1)S(1)}, bf16[128,256]{0,1:T(8,128)(2,1)}, u32[]{:S(2)}) copy-start(bf16[128,256]{0,1:T(8,128)(2,1)} %copy.51) | copy-start | bytes 196612
  401.8 418.1 %copy-start.4 = (bf16[128,256]{0,1:T(8,128)(2,1)S(1)}, bf16[128,256]{0,1:T(8,128)(2,1)}, u32[]{:S(2)}) copy-start(bf16[128,256]{0,1:T(8,128)(2,1)} %copy.49) | copy-start | bytes 196612
  518.9 301.0 %copy-start.8 = (f32[128,64]{0,1:T(8,128)}, f32[128,64]{0,1:T(8,128)S(1)}, u32[]{:S(2)}) copy-start(f32[128,64]{0,1:T(8,128)S(1)} %get-tuple-element.879) | copy-start | bytes 98308
  829.1 10.8 %copy-start.10 = (f32[8192,4]{0,1:T(4,128)S(1)}, f32[8192,4]{0,1:T(4,128)}, u32[]{:S(2)}) copy-start(f32[8192,4]{0,1:T(4,128)} %copy-done.9) | copy-start | bytes 393220 | tf_op jit(solution)/shard_map/while
  829.1 10.7 %copy-start.12 = (f32[8192,4]{0,1:T(4,128)S(1)}, f32[8192,4]{0,1:T(4,128)}, u32[]{:S(2)}) copy-start(f32[8192,4]{0,1:T(4,128)} %copy-done.11) | copy-start | bytes 393220 | tf_op jit(solution)/shard_map/while
  849.0 10.8 %copy-start.10 = (f32[8192,4]{0,1:T(4,128)S(1)}, f32[8192,4]{0,1:T(4,128)}, u32[]{:S(2)}) copy-start(f32[8192,4]{0,1:T(4,128)} %copy-done.9) | copy-start | bytes 393220 | tf_op jit(solution)/shard_map/while
  849.0 10.7 %copy-start.12 = (f32[8192,4]{0,1:T(4,128)S(1)}, f32[8192,4]{0,1:T(4,128)}, u32[]{:S(2)}) copy-start(f32[8192,4]{0,1:T(4,128)} %copy-done.11) | copy-start | bytes 393220 | tf_op jit(solution)/shard_map/while
  868.9 10.8 %copy-start.10 = (f32[8192,4]{0,1:T(4,128)S(1)}, f32[8192,4]{0,1:T(4,128)}, u32[]{:S(2)}) copy-start(f32[8192,4]{0,1:T(4,128)} %copy-done.9) | copy-start | bytes 393220 | tf_op jit(solution)/shard_map/while
  868.9 10.7 %copy-start.12 = (f32[8192,4]{0,1:T(4,128)S(1)}, f32[8192,4]{0,1:T(4,128)}, u32[]{:S(2)}) copy-start(f32[8192,4]{0,1:T(4,128)} %copy-done.11) | copy-start | bytes 393220 | tf_op jit(solution)/shard_map/while
  888.8 10.8 %copy-start.10 = (f32[8192,4]{0,1:T(4,128)S(1)}, f32[8192,4]{0,1:T(4,128)}, u32[]{:S(2)}) copy-start(f32[8192,4]{0,1:T(4,128)} %copy-done.9) | copy-start | bytes 393220 | tf_op jit(solution)/shard_map/while
  888.9 10.7 %copy-start.12 = (f32[8192,4]{0,1:T(4,128)S(1)}, f32[8192,4]{0,1:T(4,128)}, u32[]{:S(2)}) copy-start(f32[8192,4]{0,1:T(4,128)} %copy-done.11) | copy-start | bytes 393220 | tf_op jit(solution)/shard_map/while
  908.8 10.8 %copy-start.10 = (f32[8192,4]{0,1:T(4,128)S(1)}, f32[8192,4]{0,1:T(4,128)}, u32[]{:S(2)}) copy-start(f32[8192,4]{0,1:T(4,128)} %copy-done.9) | copy-start | bytes 393220 | tf_op jit(solution)/shard_map/while
  908.8 10.7 %copy-start.12 = (f32[8192,4]{0,1:T(4,128)S(1)}, f32[8192,4]{0,1:T(4,128)}, u32[]{:S(2)}) copy-start(f32[8192,4]{0,1:T(4,128)} %copy-done.11) | copy-start | bytes 393220 | tf_op jit(solution)/shard_map/while
  928.7 10.8 %copy-start.10 = (f32[8192,4]{0,1:T(4,128)S(1)}, f32[8192,4]{0,1:T(4,128)}, u32[]{:S(2)}) copy-start(f32[8192,4]{0,1:T(4,128)} %copy-done.9) | copy-start | bytes 393220 | tf_op jit(solution)/shard_map/while
  928.7 10.7 %copy-start.12 = (f32[8192,4]{0,1:T(4,128)S(1)}, f32[8192,4]{0,1:T(4,128)}, u32[]{:S(2)}) copy-start(f32[8192,4]{0,1:T(4,128)} %copy-done.11) | copy-start | bytes 393220 | tf_op jit(solution)/shard_map/while
  948.6 10.8 %copy-start.10 = (f32[8192,4]{0,1:T(4,128)S(1)}, f32[8192,4]{0,1:T(4,128)}, u32[]{:S(2)}) copy-start(f32[8192,4]{0,1:T(4,128)} %copy-done.9) | copy-start | bytes 393220 | tf_op jit(solution)/shard_map/while
  948.6 10.7 %copy-start.12 = (f32[8192,4]{0,1:T(4,128)S(1)}, f32[8192,4]{0,1:T(4,128)}, u32[]{:S(2)}) copy-start(f32[8192,4]{0,1:T(4,128)} %copy-done.11) | copy-start | bytes 393220 | tf_op jit(solution)/shard_map/while
  968.5 10.8 %copy-start.10 = (f32[8192,4]{0,1:T(4,128)S(1)}, f32[8192,4]{0,1:T(4,128)}, u32[]{:S(2)}) copy-start(f32[8192,4]{0,1:T(4,128)} %copy-done.9) | copy-start | bytes 393220 | tf_op jit(solution)/shard_map/while
  968.5 10.7 %copy-start.12 = (f32[8192,4]{0,1:T(4,128)S(1)}, f32[8192,4]{0,1:T(4,128)}, u32[]{:S(2)}) copy-start(f32[8192,4]{0,1:T(4,128)} %copy-done.11) | copy-start | bytes 393220 | tf_op jit(solution)/shard_map/while
  (88 other events, 312.3 us)
Sparse Core Ops, SparseCore 0:
  12.3 117.9 all-gather.7
  134.3 106.2 all-gather.5
  244.1 109.4 all-gather.9
  357.5 109.4 all-gather.11
  470.3 109.5 all-gather.13
where the time goes:
time: 1060 us
  blocking collectives  370 us (35%)
  waiting for transfers between devices  337 us (32%)
  matrix products  225 us (21%)
  local copies, waits for them, and re-layouts  74 us (7%)
  other arithmetic  35.5 us (3%)
  between operations  13.9 us (1%)
    all_gather x1, blocking collectives, on_device(): lax.all_gather(log_total.T, 'seq', axis=0, tiled=True)  153 us
    all_gather x1, blocking collectives, on_device(): lax.all_gather(row_delta.T, 'seq', axis=0, tiled=True)  147 us
    all_gather x1, waiting for transfers between devices, on_device(): lax.all_gather(embedding, 'seq', axis=0, tiled=True)  113 us
    all_gather x1, waiting for transfers between devices, on_device(): lax.all_gather(value_in, 'seq', axis=0, tiled=True)  113 us
    all_gather x1, waiting for transfers between devices, on_device(): lax.all_gather(key_in, 'seq', axis=0, tiled=True)  110 us
    dot_general x16, matrix products, update(): jnp.einsum('h,hqk->qk', bias_gain, grad_score, precision=lax.Precision.HI...  101 us
    psum x1, blocking collectives, on_device(): lax.psum((query_side + key_side).astype(jnp.bfloat16), 'head')  69.5 us
    dot_general x24, matrix products, distances(): jnp.dot(left, right.T, precision=lax.Precision.HIGHEST, preferred_element...  32.3 us
  transfers between devices with their start and end apart: 5, of which 3 were waited for; matrix products, arithmetic and copies ran while one was open for 16% of the time, Pallas kernels for 0%

commit v1 on v0

v1 whole, which is shorter than its diff:
```python
import functools

import jax
import jax.numpy as jnp
from jax import lax
from jax.experimental import pallas as pl
from jax.experimental.pallas import tpu as pltpu
from jax.sharding import PartitionSpec as P

MESH = pl.DeviceIdType.MESH
F32 = jnp.float32
BF16 = jnp.bfloat16
LANES = 128
TILE = 256
ONE_LANE = 76
EMB_ROWS = 80


def nt_dot(left, right):
    return lax.dot_general(left, right, (((1,), (1,)), ((), ())), preferred_element_type=F32)


def nn_dot(left, right):
    return jnp.dot(left, right, preferred_element_type=F32)


def rounded(x):
    return x.astype(BF16).astype(F32)


def three_parts(x):
    first = rounded(x)
    second = rounded(x - first)
    return first, second, rounded(x - first - second)


def gain_pattern(base, gain):
    lane = lax.broadcasted_iota(jnp.int32, (1, LANES), 1) - base
    one, two, three = three_parts(jnp.full((1, LANES), gain, F32))
    out = jnp.where((lane == 0) | (lane == 3) | (lane == 5), -one, 0.0)
    out = jnp.where((lane == 1) | (lane == 4), -two, out)
    return jnp.where(lane == 2, -three, out)


Z_FIRST = ((0, 2, 2, 0), (0, -2, 6, 0), (0, 1, 1, 0), (0, -1, 7, 0))
Z_AHEAD = ((-2, 2, 4, 1), (-2, 1, 3, 0))
Z_BACK = ((2, -2, 0, 2), (2, -1, 5, 0))
FAR_FIRST = (4, 3, 5, 2, 6, 1, 7)


def kernel(
    na, nz, nh,
    gain_ref, q_ref, k_ref, v_ref, g_ref, emb_ref,
    dq_ref, dk_ref, dv_ref, de_ref,
    qd, kv, eq, ek, ka, qa, qx, ket, eqt, emb_q, emb_k, erq, erk,
    scores, probs, w16, d16, own_max, stats, combined,
    dqt, row_emb, col_emb, dq_out, dkv_out, dq_in, dkv_in,
    emb_out, emb_in, head_out, head_in,
    gz_send, gz_recv, ga_send, ga_recv, st_send, st_recv,
    dq_send, dq_recv, dkv_send, dkv_recv, em_send, em_recv, hd_send, hd_recv,
):
    rows = q_ref.shape[0]
    heads = q_ref.shape[1] // 64
    nq, nk = nz * rows, na * rows
    nx = na // 2
    last = heads - 1
    seq, head = lax.axis_index("seq"), lax.axis_index("head")
    a, z = seq // nz, seq % nz
    y, x = a // nx, a % nx
    own_q = pl.multiple_of(z * rows, rows)
    own_k = pl.multiple_of(a * rows, rows)

    def z_at(step):
        return (z + step + nz) % nz

    def z_device(place):
        return (a * nz + place, head)

    def a_device(place):
        return (place * nz + z, head)

    barrier = pltpu.get_barrier_semaphore()

    def greet(target):
        pl.semaphore_signal(barrier, inc=1, device_id=target, device_id_type=MESH)

    for step in range(1, nz):
        greet(z_device(z_at(step)))
    for step in range(1, na):
        greet(a_device((a + step) % na))
    for step in range(1, nh):
        greet((seq, (head + step) % nh))

    eq[:, pl.ds(own_q, rows)] = emb_ref[...]
    ek[:, pl.ds(own_k, rows)] = emb_ref[...]
    for h in range(heads):
        cols = slice(h * 64, (h + 1) * 64)
        qd[h, pl.ds(own_q, rows), :] = jnp.concatenate(
            [q_ref[:, cols].astype(F32) * 0.125, g_ref[:, cols].astype(F32)], axis=1
        ).astype(BF16)
        kv[h, pl.ds(own_k, rows), :] = jnp.concatenate(
            [k_ref[:, cols].astype(F32), v_ref[:, cols].astype(F32)], axis=1
        ).astype(BF16)

    pl.semaphore_wait(barrier, (nz - 1) + (na - 1) + (nh - 1))

    def piece(msg, buffer, emb_buffer, place, part):
        at = pl.multiple_of(place * rows, rows)
        if msg is None:
            size = 64 if part == 0 else 32
            return emb_buffer.at[pl.ds(32 if part == 2 else 0, size), pl.ds(at, rows)]
        size = rows if part == 0 else rows // 2
        return buffer.at[msg, pl.ds(at + (rows // 2 if part == 2 else 0), size), :]

    def number(msg):
        return heads if msg is None else msg

    def z_send(msg, plan):
        for held, to, slot, part in plan:
            block = piece(msg, qd, eq, z_at(held), part)
            pltpu.make_async_remote_copy(
                src_ref=block, dst_ref=block,
                send_sem=gz_send.at[number(msg)], recv_sem=gz_recv.at[number(msg), slot],
                device_id=z_device(z_at(to)), device_id_type=MESH).start()

    def z_wait(msg, slot):
        block = piece(msg, qd, eq, z_at(-4 if slot == 0 else -slot), {0: 2, 4: 1}.get(slot, 0))
        pltpu.make_async_copy(block, block, gz_recv.at[number(msg), slot]).wait()

    def a_send(msg, partner):
        held = ((y + partner) % 2) * nx + x
        block = piece(msg, kv, ek, held, 0)
        targets = [] if partner else [(4, ((y + 1) % 2) * nx + x)]
        targets += [(4 * partner + step, y * nx + (x + step) % nx) for step in (2, 1, 3)]
        for slot, place in targets:
            pltpu.make_async_remote_copy(
                src_ref=block, dst_ref=block,
                send_sem=ga_send.at[number(msg)], recv_sem=ga_recv.at[number(msg), slot],
                device_id=a_device(place), device_id_type=MESH).start()

    def a_wait(msg, slot):
        held = ((y + slot // 4) % 2) * nx + (x - slot % 4 + nx) % nx
        block = piece(msg, kv, ek, held, 0)
        pltpu.make_async_copy(block, block, ga_recv.at[number(msg), slot]).wait()

    def gather_start(msg):
        a_send(msg, 0)
        z_send(msg, Z_FIRST)

    def gather_forward(msg):
        a_wait(msg, 4)
        a_send(msg, 1)
        z_wait(msg, 2)
        z_send(msg, Z_AHEAD)
        z_wait(msg, 6)
        z_send(msg, Z_BACK)

    def gather_end(msg):
        for slot in (1, 7, 3, 5, 4, 0):
            z_wait(msg, slot)
        for slot in (1, 3, 2, 5, 7, 6):
            a_wait(msg, slot)

    def spread_z(source, dest, send_sem, recv_sem):
        for step in FAR_FIRST:
            other = z_at(step)
            pltpu.make_async_remote_copy(
                src_ref=source(other), dst_ref=dest, send_sem=send_sem, recv_sem=recv_sem,
                device_id=z_device(other), device_id_type=MESH).start()

    def send_a(other, source, dest, send_sem, recv_sem):
        @pl.when(other != a)
        def _():
            pltpu.make_async_remote_copy(
                src_ref=source, dst_ref=dest, send_sem=send_sem, recv_sem=recv_sem,
                device_id=a_device(other), device_id_type=MESH).start()

    def bytes_of(block, sem):
        pltpu.make_async_copy(block, block, sem).wait()

    gather_start(None)
    gather_start(0)
    row_emb[...] = jnp.zeros_like(row_emb)
    col_emb[...] = jnp.zeros_like(col_emb)
    gather_forward(None)
    gather_forward(0)
    gather_start(1)
    gather_end(None)

    def widened(emb_t, base):
        e = emb_t.astype(F32)
        one, two, three = three_parts(jnp.sum(e * e, axis=0, keepdims=True))
        row = lax.broadcasted_iota(jnp.int32, (16, e.shape[1]), 0) + (64 - base)
        extra = jnp.where((row >= 0) & (row < 3), one, 0.0)
        extra = jnp.where((row >= 3) & (row < 5), two, extra)
        extra = jnp.where(row == 5, three, extra)
        extra = jnp.where(row == ONE_LANE - base, 1.0, extra)
        return jnp.concatenate([e, extra, jnp.zeros((48, e.shape[1]), F32)], axis=0)

    eqt[...] = widened(eq[...], 64)
    emb_q[...] = jnp.transpose(eqt[...])
    wide_k = widened(ek[...], 70)
    ket[64:, :] = wide_k[:EMB_ROWS].astype(BF16)
    emb_k[...] = jnp.transpose(wide_k)
    qx[:, LANES:] = emb_q[...].astype(BF16)
    erq[...] = pltpu.roll(emb_q[...], 64, 1)
    erk[...] = pltpu.roll(emb_k[...], 64, 1).astype(BF16)

    low_lane = lax.broadcasted_iota(jnp.int32, (1, LANES), 1) < 64
    low_f32 = jnp.where(low_lane, 1.0, 0.0)
    high_f32 = 1.0 - low_f32

    def first_pass(h):
        slot = h % 2
        gather_end(h)
        gain = gain_ref[h]
        ka[:, :LANES] = (kv[h].astype(F32) * low_f32 + erk[...].astype(F32) * high_f32).astype(BF16)
        less = jnp.where(lax.broadcasted_iota(jnp.int32, (1, LANES), 1) == ONE_LANE, -1.0, 0.0)
        ka[:, LANES:] = (emb_k[...] + (gain_pattern(64, gain) + less)).astype(BF16)
        shifted = erq[...] * (2.0 * gain)
        scaled = emb_q[...] * (2.0 * gain)
        qa[:, :LANES] = (qd[h].astype(F32) * low_f32 + rounded(shifted) * high_f32).astype(BF16)
        low_part = scaled - rounded(scaled)
        qa[:, LANES:] = (
            low_part * low_f32 + (emb_q[...] + gain_pattern(70, gain)) * high_f32
        ).astype(BF16)

        def block(qb, _):
            at = pl.multiple_of(qb * TILE, TILE)
            q_tile = qa[pl.ds(at, TILE), :]
            top = jnp.full((8, TILE), -jnp.inf, F32)
            for kb in range(nk // TILE):
                s = nt_dot(ka[kb * TILE:(kb + 1) * TILE, :], q_tile)
                scores[slot, kb * TILE:(kb + 1) * TILE, pl.ds(at, TILE)] = s
                top = jnp.maximum(top, jnp.max(s.reshape(TILE // 8, 8, TILE), axis=0))
            top = jnp.max(top, axis=0, keepdims=True)
            g_tile = (qd[h, pl.ds(at, TILE), :].astype(F32) * high_f32).astype(BF16)
            total = jnp.zeros((8, TILE), F32)
            moment = jnp.zeros((8, TILE), F32)
            for kb in range(nk // TILE):
                keys = slice(kb * TILE, (kb + 1) * TILE)
                e = jnp.exp(scores[slot, keys, pl.ds(at, TILE)] - top)
                p = nt_dot(kv[h, keys, :], g_tile)
                scores[slot, keys, pl.ds(at, TILE)] = e
                probs[slot, keys, pl.ds(at, TILE)] = p
                total = total + jnp.sum(e.reshape(TILE // 8, 8, TILE), axis=0)
                moment = moment + jnp.sum((e * p).reshape(TILE // 8, 8, TILE), axis=0)
            total = jnp.sum(total, axis=0, keepdims=True)
            moment = jnp.sum(moment, axis=0, keepdims=True) / total
            log_sum = top + jnp.log(total)
            for part in range(TILE // LANES):
                cols = slice(part * LANES, (part + 1) * LANES)
                row = qb * (TILE // LANES) + part
                own_max[slot, pl.ds(row, 1), :] = top[:, cols]
                stats[h, z, pl.ds(row, 1), :] = log_sum[:, cols]
                stats[h, z, pl.ds(row + 8, 1), :] = moment[:, cols]

            @pl.when((qb == 2) & (h < last))
            def _():
                gather_forward(h + 1)

            @pl.when((qb == 3) & (h < last - 1))
            def _():
                gather_start(h + 2)
            return 0

        lax.fori_loop(0, nq // TILE, block, 0)
        own = stats.at[h, z]
        spread_z(lambda other: own, own, st_send.at[h], st_recv.at[h])

    def second_pass(h):
        slot = h % 2
        gain = gain_ref[h]
        qx[:, :LANES] = qd[h]
        ket[:64, :] = jnp.transpose(kv[h].astype(F32))[:64].astype(BF16)
        dqt[...] = jnp.zeros_like(dqt)
        bytes_of(stats.at[h, pl.ds(0, nz - 1)], st_recv.at[h])
        top = stats[h, 0, 0:8, :]
        for other in range(1, nz):
            top = jnp.maximum(top, stats[h, other, 0:8, :])
        total = jnp.zeros((8, LANES), F32)
        moment = jnp.zeros((8, LANES), F32)
        for other in range(nz):
            share = jnp.exp(stats[h, other, 0:8, :] - top)
            total = total + share
            moment = moment + stats[h, other, 8:16, :] * share
        combined[0:8, :] = jnp.exp(own_max[slot] - top) / total
        combined[8:16, :] = moment / total

        def block(kb, _):
            at = pl.multiple_of(kb * TILE, TILE)
            for part in range(nq // LANES):
                cols = slice(part * LANES, (part + 1) * LANES)
                w = scores[slot, pl.ds(at, TILE), cols] * combined[part:part + 1, :]
                d = w * (probs[slot, pl.ds(at, TILE), cols] - combined[8 + part:9 + part, :])
                w16[:, cols] = w.astype(BF16)
                d16[:, cols] = d.astype(BF16)
            grad_v = nn_dot(w16[...], qx[:, :LANES])
            grad_k = nn_dot(d16[...], qx[...])
            dkv_out[h, pl.ds(at, TILE), :] = (
                grad_k[:, :LANES] * low_f32 + grad_v * high_f32
            ).astype(BF16)
            col_emb[pl.ds(at, TILE), :] += gain * grad_k[:, LANES:]
            for part in range(TILE // rows):
                other = kb * (TILE // rows) + part
                send_a(other, dkv_out.at[h, pl.ds(at + part * rows, rows), :], dkv_in.at[h, a],
                       dkv_send.at[h], dkv_recv.at[h])

            @pl.when(h == last)
            def _():
                col_t = jnp.transpose(col_emb[pl.ds(at, TILE), :])
                emb_out[1, :, pl.ds(at, TILE)] = (-2.0 * (
                    col_t[ONE_LANE:ONE_LANE + 1, :] * ek[:, pl.ds(at, TILE)].astype(F32)
                    - col_t[:64, :])).astype(BF16)
                for part in range(TILE // rows):
                    other = kb * (TILE // rows) + part
                    send_a(other, emb_out.at[1, :, pl.ds(at + part * rows, rows)],
                           emb_in.at[1, a], em_send.at[1], em_recv.at[1])
            dqt[...] += nn_dot(ket[:, pl.ds(at, TILE)], d16[...])
            return 0

        lax.fori_loop(0, nk // TILE, block, 0)
        row_emb[...] += gain * dqt[64:, :]

        @pl.when(h == last)
        def _():
            emb_out[0] = (-2.0 * (
                row_emb[ONE_LANE:ONE_LANE + 1, :] * eqt[:64, :] - row_emb[:64, :])).astype(BF16)
            spread_z(
                lambda other: emb_out.at[0, :, pl.ds(pl.multiple_of(other * rows, rows), rows)],
                emb_in.at[0, z], em_send.at[0], em_recv.at[0])

        dq_out[h] = (dqt[:64, :] * 0.125).astype(BF16)
        spread_z(
            lambda other: dq_out.at[h, :, pl.ds(pl.multiple_of(other * rows, rows), rows)],
            dq_in.at[h, z], dq_send.at[h], dq_recv.at[h])
        dq_in[h, z] = dq_out[h, :, pl.ds(own_q, rows)]
        dkv_in[h, a] = dkv_out[h, pl.ds(own_k, rows), :]

    def step(t, _):
        @pl.when(t < heads)
        def _():
            first_pass(t)

        @pl.when(t > 0)
        def _():
            second_pass(t - 1)
        return 0

    lax.fori_loop(0, heads + 1, step, 0)
    emb_in[0, z] = emb_out[0, :, pl.ds(own_q, rows)]
    emb_in[1, a] = emb_out[1, :, pl.ds(own_k, rows)]

    def reduce_pair(pair):
        halves = []
        for h in (2 * pair, 2 * pair + 1):
            bytes_of(dq_in.at[h, pl.ds(0, nz - 1)], dq_recv.at[h])
            bytes_of(dkv_in.at[h, pl.ds(0, na - 1)], dkv_recv.at[h])
            halves.append((
                jnp.sum(dq_in[h].astype(F32), axis=0), jnp.sum(dkv_in[h].astype(F32), axis=0)))
        cols = slice(pair * LANES, (pair + 1) * LANES)
        (q0, kv0), (q1, kv1) = halves
        dq_ref[:, cols] = jnp.transpose(jnp.concatenate([q0, q1], axis=0)).astype(BF16)
        dk_ref[:, cols] = jnp.concatenate([kv0[:, :64], kv1[:, :64]], axis=1).astype(BF16)
        dv_ref[:, cols] = jnp.concatenate([kv0[:, 64:], kv1[:, 64:]], axis=1).astype(BF16)

    def gather_sent(msg):
        whole_q, whole_k = (eq, ek) if msg is None else (qd.at[msg], kv.at[msg])
        if msg is None:
            whole_q, whole_k = eq.at[:, pl.ds(0, nq - rows)], ek.at[:, pl.ds(0, nk - rows)]
        else:
            whole_q = qd.at[msg, pl.ds(0, nq - rows), :]
            whole_k = kv.at[msg, pl.ds(0, nk - rows), :]
        bytes_of(whole_q, gz_send.at[number(msg)])
        bytes_of(whole_k, ga_send.at[number(msg)])

    for pair in range(heads // 2 - 1):
        reduce_pair(pair)
    gather_sent(None)
    for h in range(heads):
        gather_sent(h)
        bytes_of(stats.at[h, pl.ds(0, nz - 1)], st_send.at[h])
    bytes_of(emb_in.at[1, pl.ds(0, na - 1)], em_recv.at[1])
    bytes_of(emb_in.at[0, pl.ds(0, nz - 1)], em_recv.at[0])
    mine = jnp.sum(emb_in[0].astype(F32), axis=0) + jnp.sum(emb_in[1].astype(F32), axis=0)
    head_out[...] = mine
    for step in range(1, nh):
        pltpu.make_async_remote_copy(
            src_ref=head_out, dst_ref=head_in.at[head], send_sem=hd_send, recv_sem=hd_recv,
            device_id=(seq, (head + step) % nh), device_id_type=MESH).start()
    head_in[head] = mine
    reduce_pair(heads // 2 - 1)
    for h in range(heads):
        bytes_of(dq_in.at[h, pl.ds(0, nz - 1)], dq_send.at[h])
        bytes_of(dkv_in.at[h, pl.ds(0, na - 1)], dkv_send.at[h])
    bytes_of(emb_in.at[0, pl.ds(0, nz - 1)], em_send.at[0])
    bytes_of(emb_in.at[1, pl.ds(0, na - 1)], em_send.at[1])
    bytes_of(head_in.at[pl.ds(0, nh - 1)], hd_send)
    bytes_of(head_in.at[pl.ds(0, nh - 1)], hd_recv)
    de_ref[...] = jnp.sum(head_in[...], axis=0)


def on_device(na, nz, nh, query_in, key_in, value_in, grad_out, embedding, bias_gain):
    rows, width = query_in.shape
    heads = width // 64
    nq, nk = nz * rows, na * rows
    vmem = pl.BlockSpec(memory_space=pltpu.VMEM)
    dma = pltpu.SemaphoreType.DMA
    grad_q, grad_k, grad_v, grad_e = pl.pallas_call(
        functools.partial(kernel, na, nz, nh),
        out_shape=(
            jax.ShapeDtypeStruct((rows, width), BF16),
            jax.ShapeDtypeStruct((rows, width), BF16),
            jax.ShapeDtypeStruct((rows, width), BF16),
            jax.ShapeDtypeStruct((64, rows), F32),
        ),
        in_specs=[pl.BlockSpec(memory_space=pltpu.SMEM)] + [vmem] * 5,
        out_specs=(vmem,) * 4,
        scratch_shapes=[
            pltpu.VMEM((heads, nq, LANES), BF16),
            pltpu.VMEM((heads, nk, LANES), BF16),
            pltpu.VMEM((64, nq), BF16),
            pltpu.VMEM((64, nk), BF16),
            pltpu.VMEM((nk, 2 * LANES), BF16),
            pltpu.VMEM((nq, 2 * LANES), BF16),
            pltpu.VMEM((nq, 2 * LANES), BF16),
            pltpu.VMEM((64 + EMB_ROWS, nk), BF16),
            pltpu.VMEM((LANES, nq), F32),
            pltpu.VMEM((nq, LANES), F32),
            pltpu.VMEM((nk, LANES), F32),
            pltpu.VMEM((nq, LANES), F32),
            pltpu.VMEM((nk, LANES), BF16),
            pltpu.VMEM((2, nk, nq), F32),
            pltpu.VMEM((2, nk, nq), F32),
            pltpu.VMEM((TILE, nq), BF16),
            pltpu.VMEM((TILE, nq), BF16),
            pltpu.VMEM((2, 8, LANES), F32),
            pltpu.VMEM((heads, nz, 16, LANES), F32),
            pltpu.VMEM((16, LANES), F32),
            pltpu.VMEM((64 + EMB_ROWS, nq), F32),
            pltpu.VMEM((EMB_ROWS, nq), F32),
            pltpu.VMEM((nk, LANES), F32),
            pltpu.VMEM((heads, 64, nq), BF16),
            pltpu.VMEM((heads, nk, LANES), BF16),
            pltpu.VMEM((heads, nz, 64, rows), BF16),
            pltpu.VMEM((heads, na, rows, LANES), BF16),
            pltpu.VMEM((2, 64, max(nq, nk)), BF16),
            pltpu.VMEM((2, max(na, nz), 64, rows), BF16),
            pltpu.VMEM((64, rows), F32),
            pltpu.VMEM((nh, 64, rows), F32),
            dma((heads + 1,)), dma((heads + 1, nz)),
            dma((heads + 1,)), dma((heads + 1, na)),
            dma((heads,)), dma((heads,)),
            dma((heads,)), dma((heads,)),
            dma((heads,)), dma((heads,)),
            dma((2,)), dma((2,)),
            dma, dma,
        ],
        compiler_params=pltpu.CompilerParams(
            collective_id=0, has_side_effects=True, vmem_limit_bytes=56 * 1024 * 1024
        ),
    )(bias_gain, query_in, key_in, value_in, grad_out, embedding.T)
    return grad_q, grad_k, grad_v, grad_e.T


def solution(mesh):
    seq, nh = mesh.shape["seq"], mesh.shape["head"]
    nz = 1
    while nz * nz < seq:
        nz *= 2
    na = seq // nz
    placed = (
        P("seq", "head"),
        P("seq", "head"),
        P("seq", "head"),
        P("seq", "head"),
        P("seq", None),
        P("head"),
    )
    return jax.shard_map(
        functools.partial(on_device, na, nz, nh),
        mesh=mesh,
        in_specs=placed,
        out_specs=(P("seq", "head"), P("seq", "head"), P("seq", "head"), P("seq", None)),
        check_vma=False,
    )
```

time: 1060 us -> 68.6 us (0.06)
  blocking collectives: 370 us -> 0 us
  waiting for transfers between devices: 337 us -> 0 us
  matrix products: 225 us -> 0 us
  local copies, waits for them, and re-layouts: 74 us -> 3.74 us
  Pallas kernels: 0 us -> 63.9 us
  other arithmetic: 35.5 us -> 0 us
  between operations: 13.9 us -> 0.65 us
    all_gather x5 -> x0, waiting for transfers between devices: 337 us -> none  [the longest x1 113 us: on_device(): lax.all_gather(embedding, 'seq', axis=0, tiled=True)]
    all_gather x2 -> x0, blocking collectives: 300 us -> none  [the longest x1 153 us: on_device(): lax.all_gather(log_total.T, 'seq', axis=0, tiled=True)]
    dot_general x128 -> x0, matrix products: 225 us -> none  [the longest x16 101 us: update(): jnp.einsum('h,hqk->qk', bias_gain, grad_score, precision=lax.Precision.HI...]
    psum x1 -> x0, blocking collectives: 69.5 us -> none  [on_device(): lax.psum((query_side + key_side).astype(jnp.bfloat16), 'head')]
    pallas_call x0 -> x1, Pallas kernels: none -> 63.9 us  [on_device(): pl.pallas_call(functools.partial(kernel, na, nz, nh), out_shape=(jax.Shap...]
    reduce_sum x49 -> x0, other arithmetic: 33.6 us -> none  [the longest x16 18.8 us: distances(): right_sq = jnp.sum(right * right, axis=1)]
    dynamic_slice x24 -> x0, local copies, waits for them, and re-layouts: 31.8 us -> none  [advance(): lax.dynamic_slice_in_dim(piece, offset, block_rows, 0)]
    mul x8 -> x0, local copies, waits for them, and re-layouts: 16 us -> none  [update(): grad_score = weights * (grad_prob - row_delta[:, :, None])]
  transfers between devices with their start and end apart: 5 -> 0, of which waited for: 3 -> 0; matrix products, arithmetic and copies ran while one was open for 16% -> 0% of each run, Pallas kernels for 0% -> 0%
where the time goes in v1:
time: 68.6 us; the launch traced here: 68.3 us
  Pallas kernels  63.9 us (93%)
  local copies, waits for them, and re-layouts  3.74 us (5%)
    pallas_call x1, Pallas kernels, on_device(): pl.pallas_call(functools.partial(kernel, na, nz, nh), out_shape=(jax.Shap...  63.9 us
    unnamed x10, local copies, waits for them, and re-layouts  3.74 us

profile of v1, /device:TPU:1, one launch (start us, length us, event | category | flops | bytes accessed | tf_op | source)
XLA Modules:
  0.0 68.3 jit_solution(2821638657158115048)
XLA Ops:
  0.6 63.9 %shard_map.93 = (bf16[128,256]{1,0:T(8,128)(2,1)}, bf16[128,256]{1,0:T(8,128)(2,1)}, bf16[128,256]{1,0:T(8,128)(2,1)}, f32[64,128]{1,0:T(8,128)}) custom-call(f32[4]{0:T(128)} %gain_ref.1, bf16[128,256]{1,0:T(8,128)(2,1)} %q_ref.1, bf16[128,256]{1,0:T(8,128)(2,1)} %k_ref.1, bf16[128,256]{1,0:T(8,128)(2,1)} %v_ref.1, bf16[128,256]{1,0:T(8,128)(2,1)} %g_ref.1, ...), custom_call_target="tpu_custom_call" | custom-call | tf_op jit(solution)/shard_map/pallas_call | solution.py:409
  64.5 0.0 copy-start.1
  64.5 1.5 %copy.14 = bf16[128,256]{1,0:T(8,128)(2,1)} copy(bf16[128,256]{1,0:T(8,128)(2,1)} %get-tuple-element.16) | data formatting | bytes 131072
  66.0 0.0 copy-done.1
  66.0 0.0 copy-start
  66.0 0.6 copy.15
  66.7 0.2 copy-done
  66.9 0.0 copy-start.2
  66.9 0.6 copy.16
  67.5 0.1 copy-done.2
  67.6 0.6 copy.17
Async XLA Ops:
  64.5 1.5 %copy-start.1 = (bf16[128,256]{1,0:T(8,128)(2,1)S(1)}, bf16[128,256]{1,0:T(8,128)(2,1)}, u32[]{:S(2)}) copy-start(bf16[128,256]{1,0:T(8,128)(2,1)} %get-tuple-element.17) | copy-start | bytes 196612
  66.0 0.9 %copy-start = (bf16[128,256]{1,0:T(8,128)(2,1)S(1)}, bf16[128,256]{1,0:T(8,128)(2,1)}, u32[]{:S(2)}) copy-start(bf16[128,256]{1,0:T(8,128)(2,1)} %get-tuple-element.18) | copy-start | bytes 196612
  66.9 0.8 %copy-start.2 = (f32[64,128]{1,0:T(8,128)S(1)}, f32[64,128]{1,0:T(8,128)}, u32[]{:S(2)}) copy-start(f32[64,128]{1,0:T(8,128)} %get-tuple-element.11) | copy-start | bytes 98308

commit v2 on v1

--- a/solution.py
+++ b/solution.py
@@ -13,6 +13,7 @@
 LANES = 128
 TILE = 256
 ONE_LANE = 76
+SLOTS = 3
 EMB_ROWS = 80
 
 
@@ -52,9 +53,10 @@
     na, nz, nh,
     gain_ref, q_ref, k_ref, v_ref, g_ref, emb_ref,
     dq_ref, dk_ref, dv_ref, de_ref,
-    qd, kv, eq, ek, ka, qa, qx, ket, eqt, emb_q, emb_k, erq, erk,
-    scores, probs, w16, d16, own_max, stats, combined,
-    dqt, row_emb, col_emb, dq_out, dkv_out, dq_in, dkv_in,
+    q_in, k_in, v_in, g_in, emb_in_place, in_sem,
+    qd, kv, eq, ek, ka, qa, gq, qx, ket, eqt, twice_q, tail_q, tail_k,
+    scores, probs, wd16, block_max, totals, moments, shares, stats, combined,
+    row_emb, col_emb, dq_out, dkv_out, dq_in, dkv_in,
     emb_out, emb_in, head_out, head_in,
     gz_send, gz_recv, ga_send, ga_recv, st_send, st_recv,
     dq_send, dq_recv, dkv_send, dkv_recv, em_send, em_recv, hd_send, hd_recv,
@@ -91,15 +93,25 @@
     for step in range(1, nh):
         greet((seq, (head + step) % nh))
 
-    eq[:, pl.ds(own_q, rows)] = emb_ref[...]
-    ek[:, pl.ds(own_k, rows)] = emb_ref[...]
+    loads = [
+        pltpu.make_async_copy(source, dest, in_sem.at[i])
+        for i, (source, dest) in enumerate((
+            (emb_ref, emb_in_place), (q_ref, q_in), (g_ref, g_in), (k_ref, k_in), (v_ref, v_in)))
+    ]
+    for load in loads:
+        load.start()
+    for load in loads:
+        load.wait()
+
+    eq[:, pl.ds(own_q, rows)] = emb_in_place[...]
+    ek[:, pl.ds(own_k, rows)] = emb_in_place[...]
     for h in range(heads):
         cols = slice(h * 64, (h + 1) * 64)
         qd[h, pl.ds(own_q, rows), :] = jnp.concatenate(
-            [q_ref[:, cols].astype(F32) * 0.125, g_ref[:, cols].astype(F32)], axis=1
+            [q_in[:, cols].astype(F32) * 0.125, g_in[:, cols].astype(F32)], axis=1
         ).astype(BF16)
         kv[h, pl.ds(own_k, rows), :] = jnp.concatenate(
-            [k_ref[:, cols].astype(F32), v_ref[:, cols].astype(F32)], axis=1
+            [k_in[:, cols].astype(F32), v_in[:, cols].astype(F32)], axis=1
         ).astype(BF16)
 
     pl.semaphore_wait(barrier, (nz - 1) + (na - 1) + (nh - 1))
@@ -185,6 +197,7 @@
     gather_forward(None)
     gather_forward(0)
     gather_start(1)
+    gather_start(2)
     gather_end(None)
 
     def widened(emb_t, base):
@@ -197,83 +210,83 @@
         extra = jnp.where(row == ONE_LANE - base, 1.0, extra)
         return jnp.concatenate([e, extra, jnp.zeros((48, e.shape[1]), F32)], axis=0)
 
-    eqt[...] = widened(eq[...], 64)
-    emb_q[...] = jnp.transpose(eqt[...])
-    wide_k = widened(ek[...], 70)
-    ket[64:, :] = wide_k[:EMB_ROWS].astype(BF16)
-    emb_k[...] = jnp.transpose(wide_k)
-    qx[:, LANES:] = emb_q[...].astype(BF16)
-    erq[...] = pltpu.roll(emb_q[...], 64, 1)
-    erk[...] = pltpu.roll(emb_k[...], 64, 1).astype(BF16)
-
     low_lane = lax.broadcasted_iota(jnp.int32, (1, LANES), 1) < 64
     low_f32 = jnp.where(low_lane, 1.0, 0.0)
     high_f32 = 1.0 - low_f32
+    low_16, high_16 = low_f32.astype(BF16), high_f32.astype(BF16)
+    one_lane = jnp.where(lax.broadcasted_iota(jnp.int32, (1, LANES), 1) == ONE_LANE, 1.0, 0.0)
+
+    eqt[...] = widened(eq[...], 64)
+    wide_k = widened(ek[...], 70)
+    ket[64:, :] = wide_k[:EMB_ROWS].astype(BF16)
+    wide_q = jnp.transpose(eqt[...])
+    wide_k = jnp.transpose(wide_k)
+    qx[:, LANES:] = wide_q.astype(BF16)
+    tail_q[...] = (wide_q * high_f32).astype(BF16)
+    tail_k[...] = ((wide_k - one_lane) * high_f32).astype(BF16)
+    wide_q, wide_k = wide_q * low_f32, wide_k * low_f32
+    twice_q[...] = wide_q + pltpu.roll(wide_q, 64, 1)
+    ka[:, LANES:] = (wide_k + pltpu.roll(wide_k, 64, 1)).astype(BF16)
 
     def first_pass(h):
-        slot = h % 2
-        gather_end(h)
+        slot = h % SLOTS
+        @pl.when(h > 0)
+        def _():
+            gather_end(h)
+
         gain = gain_ref[h]
-        ka[:, :LANES] = (kv[h].astype(F32) * low_f32 + erk[...].astype(F32) * high_f32).astype(BF16)
-        less = jnp.where(lax.broadcasted_iota(jnp.int32, (1, LANES), 1) == ONE_LANE, -1.0, 0.0)
-        ka[:, LANES:] = (emb_k[...] + (gain_pattern(64, gain) + less)).astype(BF16)
-        shifted = erq[...] * (2.0 * gain)
-        scaled = emb_q[...] * (2.0 * gain)
-        qa[:, :LANES] = (qd[h].astype(F32) * low_f32 + rounded(shifted) * high_f32).astype(BF16)
-        low_part = scaled - rounded(scaled)
-        qa[:, LANES:] = (
-            low_part * low_f32 + (emb_q[...] + gain_pattern(70, gain)) * high_f32
-        ).astype(BF16)
-
-        def block(qb, _):
-            at = pl.multiple_of(qb * TILE, TILE)
-            q_tile = qa[pl.ds(at, TILE), :]
-            top = jnp.full((8, TILE), -jnp.inf, F32)
-            for kb in range(nk // TILE):
-                s = nt_dot(ka[kb * TILE:(kb + 1) * TILE, :], q_tile)
-                scores[slot, kb * TILE:(kb + 1) * TILE, pl.ds(at, TILE)] = s
-                top = jnp.maximum(top, jnp.max(s.reshape(TILE // 8, 8, TILE), axis=0))
-            top = jnp.max(top, axis=0, keepdims=True)
-            g_tile = (qd[h, pl.ds(at, TILE), :].astype(F32) * high_f32).astype(BF16)
-            total = jnp.zeros((8, TILE), F32)
-            moment = jnp.zeros((8, TILE), F32)
-            for kb in range(nk // TILE):
-                keys = slice(kb * TILE, (kb + 1) * TILE)
-                e = jnp.exp(scores[slot, keys, pl.ds(at, TILE)] - top)
+        ka[:, :LANES] = kv[h] * low_16 + (tail_k[...] + gain_pattern(64, gain).astype(BF16))
+        qa[:, :LANES] = qd[h] * low_16 + (tail_q[...] + gain_pattern(70, gain).astype(BF16))
+        scaled = twice_q[...] * (2.0 * gain)
+        first = rounded(scaled)
+        qa[:, LANES:] = jnp.where(low_lane, first, scaled - first).astype(BF16)
+        gq[...] = qd[h] * high_16
+
+        def block(qb):
+            at = slice(qb * TILE, (qb + 1) * TILE)
+            q_tile, g_tile = qa[at, :], gq[at, :]
+            for kb in range(na):
+                keys = slice(kb * rows, (kb + 1) * rows)
+                s = nt_dot(ka[keys, :], q_tile)
                 p = nt_dot(kv[h, keys, :], g_tile)
-                scores[slot, keys, pl.ds(at, TILE)] = e
-                probs[slot, keys, pl.ds(at, TILE)] = p
-                total = total + jnp.sum(e.reshape(TILE // 8, 8, TILE), axis=0)
-                moment = moment + jnp.sum((e * p).reshape(TILE // 8, 8, TILE), axis=0)
-            total = jnp.sum(total, axis=0, keepdims=True)
-            moment = jnp.sum(moment, axis=0, keepdims=True) / total
-            log_sum = top + jnp.log(total)
-            for part in range(TILE // LANES):
-                cols = slice(part * LANES, (part + 1) * LANES)
-                row = qb * (TILE // LANES) + part
-                own_max[slot, pl.ds(row, 1), :] = top[:, cols]
-                stats[h, z, pl.ds(row, 1), :] = log_sum[:, cols]
-                stats[h, z, pl.ds(row + 8, 1), :] = moment[:, cols]
-
-            @pl.when((qb == 2) & (h < last))
-            def _():
-                gather_forward(h + 1)
-
-            @pl.when((qb == 3) & (h < last - 1))
-            def _():
-                gather_start(h + 2)
-            return 0
-
-        lax.fori_loop(0, nq // TILE, block, 0)
+                top = jnp.max(jnp.max(s.reshape(rows // 8, 8, TILE), axis=0), axis=0, keepdims=True)
+                e = jnp.exp(s - top)
+                scores[slot, keys, at] = e
+                probs[slot, keys, at] = p
+                block_max[slot, kb:kb + 1, at] = top
+                totals[kb, :, at] = jnp.sum(e.reshape(rows // 8, 8, TILE), axis=0)
+                moments[kb, :, at] = jnp.sum((e * p).reshape(rows // 8, 8, TILE), axis=0)
+
+        for qb in range(nq // TILE):
+            block(qb)
+            if qb == 2:
+                @pl.when(h < last - 1)
+                def _():
+                    gather_forward(h + 2)
+
+                @pl.when(h < last - 2)
+                def _():
+                    gather_start(h + 3)
+
+        top = jnp.max(block_max[slot], axis=0, keepdims=True)
+        share = jnp.exp(block_max[slot] - top)
+        total = sum(totals[kb] * share[kb:kb + 1] for kb in range(na))
+        moment = sum(moments[kb] * share[kb:kb + 1] for kb in range(na))
+        total = jnp.sum(total, axis=0, keepdims=True)
+        moment = jnp.sum(moment, axis=0, keepdims=True) / total
+        log_sum = top + jnp.log(total)
+        for row in range(nz):
+            cols = slice(row * rows, (row + 1) * rows)
+            stats[h, z, row:row + 1, :] = log_sum[:, cols]
+            stats[h, z, row + 8:row + 9, :] = moment[:, cols]
         own = stats.at[h, z]
         spread_z(lambda other: own, own, st_send.at[h], st_recv.at[h])
 
-    def second_pass(h):
-        slot = h % 2
+    def second_pass(h, final):
+        slot = h % SLOTS
         gain = gain_ref[h]
         qx[:, :LANES] = qd[h]
         ket[:64, :] = jnp.transpose(kv[h].astype(F32))[:64].astype(BF16)
-        dqt[...] = jnp.zeros_like(dqt)
         bytes_of(stats.at[h, pl.ds(0, nz - 1)], st_recv.at[h])
         top = stats[h, 0, 0:8, :]
         for other in range(1, nz):
@@ -284,56 +297,73 @@
             share = jnp.exp(stats[h, other, 0:8, :] - top)
             total = total + share
             moment = moment + stats[h, other, 8:16, :] * share
-        combined[0:8, :] = jnp.exp(own_max[slot] - top) / total
+        combined[0:8, :] = top + jnp.log(total)
         combined[8:16, :] = moment / total
 
-        def block(kb, _):
-            at = pl.multiple_of(kb * TILE, TILE)
-            for part in range(nq // LANES):
-                cols = slice(part * LANES, (part + 1) * LANES)
-                w = scores[slot, pl.ds(at, TILE), cols] * combined[part:part + 1, :]
-                d = w * (probs[slot, pl.ds(at, TILE), cols] - combined[8 + part:9 + part, :])
-                w16[:, cols] = w.astype(BF16)
-                d16[:, cols] = d.astype(BF16)
-            grad_v = nn_dot(w16[...], qx[:, :LANES])
-            grad_k = nn_dot(d16[...], qx[...])
-            dkv_out[h, pl.ds(at, TILE), :] = (
-                grad_k[:, :LANES] * low_f32 + grad_v * high_f32
-            ).astype(BF16)
-            col_emb[pl.ds(at, TILE), :] += gain * grad_k[:, LANES:]
-            for part in range(TILE // rows):
-                other = kb * (TILE // rows) + part
-                send_a(other, dkv_out.at[h, pl.ds(at + part * rows, rows), :], dkv_in.at[h, a],
-                       dkv_send.at[h], dkv_recv.at[h])
-
-            @pl.when(h == last)
-            def _():
-                col_t = jnp.transpose(col_emb[pl.ds(at, TILE), :])
-                emb_out[1, :, pl.ds(at, TILE)] = (-2.0 * (
-                    col_t[ONE_LANE:ONE_LANE + 1, :] * ek[:, pl.ds(at, TILE)].astype(F32)
-                    - col_t[:64, :])).astype(BF16)
-                for part in range(TILE // rows):
-                    other = kb * (TILE // rows) + part
-                    send_a(other, emb_out.at[1, :, pl.ds(at + part * rows, rows)],
-                           emb_in.at[1, a], em_send.at[1], em_recv.at[1])
-            dqt[...] += nn_dot(ket[:, pl.ds(at, TILE)], d16[...])
-            return 0
-
-        lax.fori_loop(0, nk // TILE, block, 0)
-        row_emb[...] += gain * dqt[64:, :]
-
-        @pl.when(h == last)
-        def _():
+        log_total = jnp.concatenate([combined[row:row + 1, :] for row in range(nz)], axis=1)
+        delta_row = jnp.concatenate([combined[8 + row:9 + row, :] for row in range(nz)], axis=1)
+        shares[...] = jnp.exp(block_max[slot] - log_total)
+
+        def query_block(qb):
+            at = slice(qb * TILE, (qb + 1) * TILE)
+            delta = delta_row[:, at]
+            for kb in range(na):
+                keys = slice(kb * rows, (kb + 1) * rows)
+                w = scores[slot, keys, at] * shares[kb:kb + 1, at]
+                d = w * (probs[slot, keys, at] - delta)
+                wd16[2 * kb * rows:(2 * kb + 1) * rows, at] = w.astype(BF16)
+                wd16[(2 * kb + 1) * rows:(2 * kb + 2) * rows, at] = d.astype(BF16)
+            dqt = jnp.zeros((64 + EMB_ROWS, TILE), F32)
+            for kb in range(nk // TILE):
+                d_tile = jnp.concatenate([
+                    wd16[(2 * b + 1) * rows:(2 * b + 2) * rows, at]
+                    for b in range(kb * TILE // rows, (kb + 1) * TILE // rows)], axis=0)
+                dqt = dqt + nn_dot(ket[:, kb * TILE:(kb + 1) * TILE], d_tile)
+            row_emb[:, at] += gain * dqt[64:, :]
+            dq_out[h, :, at] = (dqt[:64, :] * 0.125).astype(BF16)
+
+        for qb in range(nq // TILE):
+            query_block(qb)
+        if final:
             emb_out[0] = (-2.0 * (
-                row_emb[ONE_LANE:ONE_LANE + 1, :] * eqt[:64, :] - row_emb[:64, :])).astype(BF16)
+                row_emb[ONE_LANE:ONE_LANE + 1, :] * eqt[:64, :] - row_emb[:64, :]
+            )).astype(BF16)
             spread_z(
                 lambda other: emb_out.at[0, :, pl.ds(pl.multiple_of(other * rows, rows), rows)],
                 emb_in.at[0, z], em_send.at[0], em_recv.at[0])
-
-        dq_out[h] = (dqt[:64, :] * 0.125).astype(BF16)
         spread_z(
             lambda other: dq_out.at[h, :, pl.ds(pl.multiple_of(other * rows, rows), rows)],
             dq_in.at[h, z], dq_send.at[h], dq_recv.at[h])
+
+        for kb in range(nk // TILE):
+            at = kb * TILE
+            both = nn_dot(wd16[2 * at:2 * (at + TILE), :], qx[...])
+            for part in range(TILE // rows):
+                here = slice(at + part * rows, at + (part + 1) * rows)
+                grad_v = both[2 * part * rows:(2 * part + 1) * rows, :LANES]
+                grad_k = both[(2 * part + 1) * rows:(2 * part + 2) * rows]
+                dkv_out[h, here, :] = jnp.where(low_lane, grad_k[:, :LANES], grad_v).astype(BF16)
+                col_emb[here, :] += gain * grad_k[:, LANES:]
+            if final:
+                here = slice(at, at + TILE)
+                col_t = jnp.transpose(col_emb[here, :])
+                emb_out[1, :, here] = (-2.0 * (
+                    col_t[ONE_LANE:ONE_LANE + 1, :] * ek[:, here].astype(F32) - col_t[:64, :]
+                )).astype(BF16)
+                for part in range(TILE // rows):
+                    other = kb * (TILE // rows) + part
+                    here = pl.ds(at + part * rows, rows)
+                    send_a(other, emb_out.at[1, :, here], emb_in.at[1, a],
+                           em_send.at[1], em_recv.at[1])
+                    send_a(other, dkv_out.at[h, here, :], dkv_in.at[h, a],
+                           dkv_send.at[h], dkv_recv.at[h])
+        if not final:
+            for step in range(1, na):
+                other = (a + step) % na
+                pltpu.make_async_remote_copy(
+                    src_ref=dkv_out.at[h, pl.ds(pl.multiple_of(other * rows, rows), rows), :],
+                    dst_ref=dkv_in.at[h, a], send_sem=dkv_send.at[h], recv_sem=dkv_recv.at[h],
+                    device_id=a_device(other), device_id_type=MESH).start()
         dq_in[h, z] = dq_out[h, :, pl.ds(own_q, rows)]
         dkv_in[h, a] = dkv_out[h, pl.ds(own_k, rows), :]
 
@@ -342,12 +372,15 @@
         def _():
             first_pass(t)
 
-        @pl.when(t > 0)
+        @pl.when(t > 1)
         def _():
-            second_pass(t - 1)
+            second_pass(t - 2, False)
         return 0
 
+    gather_end(0)
+    gather_forward(1)
     lax.fori_loop(0, heads + 1, step, 0)
+    second_pass(last, True)
     emb_in[0, z] = emb_out[0, :, pl.ds(own_q, rows)]
     emb_in[1, a] = emb_out[1, :, pl.ds(own_k, rows)]
 
@@ -400,6 +433,11 @@
     de_ref[...] = jnp.sum(head_in[...], axis=0)
 
 
+def hand_over(*refs):
+    for source, dest in zip(refs[:4], refs[4:]):
+        dest[...] = source[...]
+
+
 def on_device(na, nz, nh, query_in, key_in, value_in, grad_out, embedding, bias_gain):
     rows, width = query_in.shape
     heads = width // 64
@@ -414,30 +452,37 @@
             jax.ShapeDtypeStruct((rows, width), BF16),
             jax.ShapeDtypeStruct((64, rows), F32),
         ),
-        in_specs=[pl.BlockSpec(memory_space=pltpu.SMEM)] + [vmem] * 5,
+        in_specs=[pl.BlockSpec(memory_space=pltpu.SMEM)] + [pl.BlockSpec(memory_space=pl.ANY)] * 5,
         out_specs=(vmem,) * 4,
         scratch_shapes=[
+            pltpu.VMEM((rows, width), BF16),
+            pltpu.VMEM((rows, width), BF16),
+            pltpu.VMEM((rows, width), BF16),
+            pltpu.VMEM((rows, width), BF16),
+            pltpu.VMEM((64, rows), BF16),
+            dma((5,)),
             pltpu.VMEM((heads, nq, LANES), BF16),
             pltpu.VMEM((heads, nk, LANES), BF16),
             pltpu.VMEM((64, nq), BF16),
             pltpu.VMEM((64, nk), BF16),
             pltpu.VMEM((nk, 2 * LANES), BF16),
             pltpu.VMEM((nq, 2 * LANES), BF16),
+            pltpu.VMEM((nq, LANES), BF16),
             pltpu.VMEM((nq, 2 * LANES), BF16),
             pltpu.VMEM((64 + EMB_ROWS, nk), BF16),
             pltpu.VMEM((LANES, nq), F32),
             pltpu.VMEM((nq, LANES), F32),
-            pltpu.VMEM((nk, LANES), F32),
-            pltpu.VMEM((nq, LANES), F32),
+            pltpu.VMEM((nq, LANES), BF16),
             pltpu.VMEM((nk, LANES), BF16),
-            pltpu.VMEM((2, nk, nq), F32),
-            pltpu.VMEM((2, nk, nq), F32),
-            pltpu.VMEM((TILE, nq), BF16),
-            pltpu.VMEM((TILE, nq), BF16),
-            pltpu.VMEM((2, 8, LANES), F32),
+            pltpu.VMEM((SLOTS, nk, nq), F32),
+            pltpu.VMEM((SLOTS, nk, nq), F32),
+            pltpu.VMEM((2 * nk, nq), BF16),
+            pltpu.VMEM((SLOTS, na, nq), F32),
+            pltpu.VMEM((na, 8, nq), F32),
+            pltpu.VMEM((na, 8, nq), F32),
+            pltpu.VMEM((na, nq), F32),
             pltpu.VMEM((heads, nz, 16, LANES), F32),
             pltpu.VMEM((16, LANES), F32),
-            pltpu.VMEM((64 + EMB_ROWS, nq), F32),
             pltpu.VMEM((EMB_ROWS, nq), F32),
             pltpu.VMEM((nk, LANES), F32),
             pltpu.VMEM((heads, 64, nq), BF16),
@@ -460,6 +505,13 @@
             collective_id=0, has_side_effects=True, vmem_limit_bytes=56 * 1024 * 1024
         ),
     )(bias_gain, query_in, key_in, value_in, grad_out, embedding.T)
+    results = (grad_q, grad_k, grad_v, grad_e)
+    grad_q, grad_k, grad_v, grad_e = pl.pallas_call(
+        hand_over,
+        out_shape=tuple(jax.ShapeDtypeStruct(r.shape, r.dtype) for r in results),
+        in_specs=[vmem] * 4,
+        out_specs=(vmem,) * 4,
+    )(*results)
     return grad_q, grad_k, grad_v, grad_e.T
 
 

time: 68.6 us -> 58.5 us (0.85)
  Pallas kernels: 63.9 us -> 57.6 us
  local copies, waits for them, and re-layouts: 3.74 us -> 0 us
    pallas_call x1, Pallas kernels: 63.9 us -> 56 us  [on_device(): pl.pallas_call(functools.partial(kernel, na, nz, nh), out_shape=(jax.Shap...]
    unnamed x10 -> x0, local copies, waits for them, and re-layouts: 3.74 us -> none
    pallas_call x0 -> x1, Pallas kernels: none -> 1.59 us  [on_device(): pl.pallas_call(hand_over, out_shape=tuple((jax.ShapeDtypeStruct(r.shape,...]
where the time goes in v2:
time: 58.5 us; the launch traced here: 58.2 us
  Pallas kernels  57.6 us (98%)
  between operations  0.64 us (1%)
    pallas_call x1, Pallas kernels, on_device(): pl.pallas_call(functools.partial(kernel, na, nz, nh), out_shape=(jax.Shap...  56 us
    pallas_call x1, Pallas kernels, on_device(): pl.pallas_call(hand_over, out_shape=tuple((jax.ShapeDtypeStruct(r.shape,...  1.59 us

profile of v2, /device:TPU:1, one launch (start us, length us, event | category | flops | bytes accessed | tf_op | source)
XLA Modules:
  0.0 58.2 jit_solution(18156971765983794852)
XLA Ops:
  0.6 56.0 %shard_map.93 = (bf16[128,256]{1,0:T(8,128)(2,1)}, bf16[128,256]{1,0:T(8,128)(2,1)}, bf16[128,256]{1,0:T(8,128)(2,1)}, f32[64,128]{1,0:T(8,128)}) custom-call(f32[4]{0:T(128)} %gain_ref.1, bf16[128,256]{1,0:T(8,128)(2,1)} %q_ref.1, bf16[128,256]{1,0:T(8,128)(2,1)} %k_ref.1, bf16[128,256]{1,0:T(8,128)(2,1)} %v_ref.1, bf16[128,256]{1,0:T(8,128)(2,1)} %g_ref.1, ...), custom_call_target="tpu_custom_call" | custom-call | tf_op jit(solution)/shard_map/pallas_call | solution.py:447
  56.6 1.6 %shard_map.94 = (bf16[128,256]{1,0:T(8,128)(2,1)}, bf16[128,256]{1,0:T(8,128)(2,1)}, bf16[128,256]{1,0:T(8,128)(2,1)}, f32[64,128]{1,0:T(8,128)}) custom-call(bf16[128,256]{1,0:T(8,128)(2,1)} %get-tuple-element.12.refs_0_, bf16[128,256]{1,0:T(8,128)(2,1)} %get-tuple-element.13.refs_1_, bf16[128,256]{1,0:T(8,128)(2,1)} %get-tuple-element.14.refs_2_, ...), custom_call_target="tpu_custom_call" | custom-call | tf_op jit(solution)/shard_map/pallas_call | solution.py:509

commit v3 on v2

--- a/solution.py
+++ b/solution.py
@@ -54,7 +54,7 @@
     gain_ref, q_ref, k_ref, v_ref, g_ref, emb_ref,
     dq_ref, dk_ref, dv_ref, de_ref,
     q_in, k_in, v_in, g_in, emb_in_place, in_sem,
-    qd, kv, eq, ek, ka, qa, gq, qx, ket, eqt, twice_q, tail_q, tail_k,
+    qbuf, kbuf, ka, qa, gq, qx, ket, eqt, twice_q, tail_q, tail_k,
     scores, probs, wd16, block_max, totals, moments, shares, stats, combined,
     row_emb, col_emb, dq_out, dkv_out, dq_in, dkv_in,
     emb_out, emb_in, head_out, head_in,
@@ -100,64 +100,69 @@
     ]
     for load in loads:
         load.start()
+
+    def head_rows(h):
+        return pl.ds(pl.multiple_of(64 + h * rows, 64), rows)
+
+    def packed(left, right, h, scale):
+        cols = slice(h * 64, (h + 1) * 64)
+        return jnp.concatenate(
+            [left[:, cols].astype(F32) * scale, right[:, cols].astype(F32)], axis=1).astype(BF16)
+
+    def pack_head(h):
+        qbuf[z, head_rows(h), :] = packed(q_in, g_in, h, 0.125)
+        kbuf[a, head_rows(h), :] = packed(k_in, v_in, h, 1.0)
+
     for load in loads:
         load.wait()
-
-    eq[:, pl.ds(own_q, rows)] = emb_in_place[...]
-    ek[:, pl.ds(own_k, rows)] = emb_in_place[...]
-    for h in range(heads):
-        cols = slice(h * 64, (h + 1) * 64)
-        qd[h, pl.ds(own_q, rows), :] = jnp.concatenate(
-            [q_in[:, cols].astype(F32) * 0.125, g_in[:, cols].astype(F32)], axis=1
-        ).astype(BF16)
-        kv[h, pl.ds(own_k, rows), :] = jnp.concatenate(
-            [k_in[:, cols].astype(F32), v_in[:, cols].astype(F32)], axis=1
-        ).astype(BF16)
+    qbuf[z, 0:64, :] = emb_in_place[...]
+    kbuf[a, 0:64, :] = emb_in_place[...]
+    pack_head(0)
 
     pl.semaphore_wait(barrier, (nz - 1) + (na - 1) + (nh - 1))
 
-    def piece(msg, buffer, emb_buffer, place, part):
-        at = pl.multiple_of(place * rows, rows)
-        if msg is None:
-            size = 64 if part == 0 else 32
-            return emb_buffer.at[pl.ds(32 if part == 2 else 0, size), pl.ds(at, rows)]
-        size = rows if part == 0 else rows // 2
-        return buffer.at[msg, pl.ds(at + (rows // 2 if part == 2 else 0), size), :]
-
-    def number(msg):
-        return heads if msg is None else msg
+    def piece(msg, buffer, place, part):
+        if isinstance(msg, int) and msg == 0:
+            first, size = 0, 64 + rows
+        else:
+            first, size = pl.multiple_of(64 + msg * rows, 64), rows
+        if part:
+            size = size // 2
+            first = first + (size if part == 2 else 0)
+        return buffer.at[place, pl.ds(first, size), :]
 
     def z_send(msg, plan):
         for held, to, slot, part in plan:
-            block = piece(msg, qd, eq, z_at(held), part)
+            block = piece(msg, qbuf, z_at(held), part)
             pltpu.make_async_remote_copy(
                 src_ref=block, dst_ref=block,
-                send_sem=gz_send.at[number(msg)], recv_sem=gz_recv.at[number(msg), slot],
+                send_sem=gz_send.at[msg], recv_sem=gz_recv.at[msg, slot],
                 device_id=z_device(z_at(to)), device_id_type=MESH).start()
 
     def z_wait(msg, slot):
-        block = piece(msg, qd, eq, z_at(-4 if slot == 0 else -slot), {0: 2, 4: 1}.get(slot, 0))
-        pltpu.make_async_copy(block, block, gz_recv.at[number(msg), slot]).wait()
+        block = piece(msg, qbuf, z_at(-4 if slot == 0 else -slot), {0: 2, 4: 1}.get(slot, 0))
+        pltpu.make_async_copy(block, block, gz_recv.at[msg, slot]).wait()
 
     def a_send(msg, partner):
         held = ((y + partner) % 2) * nx + x
-        block = piece(msg, kv, ek, held, 0)
+        block = piece(msg, kbuf, held, 0)
         targets = [] if partner else [(4, ((y + 1) % 2) * nx + x)]
         targets += [(4 * partner + step, y * nx + (x + step) % nx) for step in (2, 1, 3)]
         for slot, place in targets:
             pltpu.make_async_remote_copy(
                 src_ref=block, dst_ref=block,
-                send_sem=ga_send.at[number(msg)], recv_sem=ga_recv.at[number(msg), slot],
+                send_sem=ga_send.at[msg], recv_sem=ga_recv.at[msg, slot],
                 device_id=a_device(place), device_id_type=MESH).start()
 
     def a_wait(msg, slot):
         held = ((y + slot // 4) % 2) * nx + (x - slot % 4 + nx) % nx
-        block = piece(msg, kv, ek, held, 0)
-        pltpu.make_async_copy(block, block, ga_recv.at[number(msg), slot]).wait()
+        block = piece(msg, kbuf, held, 0)
+        pltpu.make_async_copy(block, block, ga_recv.at[msg, slot]).wait()
 
     def gather_start(msg):
+        z_send(msg, Z_FIRST[:2])
         a_send(msg, 0)
-        z_send(msg, Z_FIRST)
+        z_send(msg, Z_FIRST[2:])
 
     def gather_forward(msg):
         a_wait(msg, 4)
@@ -190,15 +195,24 @@
     def bytes_of(block, sem):
         pltpu.make_async_copy(block, block, sem).wait()
 
-    gather_start(None)
     gather_start(0)
+    pack_head(1)
+    gather_start(1)
+    for h in range(2, heads):
+        pack_head(h)
     row_emb[...] = jnp.zeros_like(row_emb)
     col_emb[...] = jnp.zeros_like(col_emb)
-    gather_forward(None)
     gather_forward(0)
-    gather_start(1)
     gather_start(2)
-    gather_end(None)
+    gather_forward(1)
+    gather_start(3)
+    gather_end(0)
+
+    def of_queries(h):
+        return qbuf[:, head_rows(h), :].reshape(nq, LANES)
+
+    def of_keys(h):
+        return kbuf[:, head_rows(h), :].reshape(nk, LANES)
 
     def widened(emb_t, base):
         e = emb_t.astype(F32)
@@ -216,8 +230,8 @@
     low_16, high_16 = low_f32.astype(BF16), high_f32.astype(BF16)
     one_lane = jnp.where(lax.broadcasted_iota(jnp.int32, (1, LANES), 1) == ONE_LANE, 1.0, 0.0)
 
-    eqt[...] = widened(eq[...], 64)
-    wide_k = widened(ek[...], 70)
+    eqt[...] = widened(jnp.concatenate([qbuf[i, 0:64, :] for i in range(nz)], axis=1), 64)
+    wide_k = widened(jnp.concatenate([kbuf[i, 0:64, :] for i in range(na)], axis=1), 70)
     ket[64:, :] = wide_k[:EMB_ROWS].astype(BF16)
     wide_q = jnp.transpose(eqt[...])
     wide_k = jnp.transpose(wide_k)
@@ -235,12 +249,12 @@
             gather_end(h)
 
         gain = gain_ref[h]
-        ka[:, :LANES] = kv[h] * low_16 + (tail_k[...] + gain_pattern(64, gain).astype(BF16))
-        qa[:, :LANES] = qd[h] * low_16 + (tail_q[...] + gain_pattern(70, gain).astype(BF16))
+        ka[:, :LANES] = of_keys(h) * low_16 + (tail_k[...] + gain_pattern(64, gain).astype(BF16))
+        qa[:, :LANES] = of_queries(h) * low_16 + (tail_q[...] + gain_pattern(70, gain).astype(BF16))
         scaled = twice_q[...] * (2.0 * gain)
         first = rounded(scaled)
         qa[:, LANES:] = jnp.where(low_lane, first, scaled - first).astype(BF16)
-        gq[...] = qd[h] * high_16
+        gq[...] = of_queries(h) * high_16
 
         def block(qb):
             at = slice(qb * TILE, (qb + 1) * TILE)
@@ -248,7 +262,7 @@
             for kb in range(na):
                 keys = slice(kb * rows, (kb + 1) * rows)
                 s = nt_dot(ka[keys, :], q_tile)
-                p = nt_dot(kv[h, keys, :], g_tile)
+                p = nt_dot(kbuf[kb, head_rows(h), :], g_tile)
                 top = jnp.max(jnp.max(s.reshape(rows // 8, 8, TILE), axis=0), axis=0, keepdims=True)
                 e = jnp.exp(s - top)
                 scores[slot, keys, at] = e
@@ -259,14 +273,10 @@
 
         for qb in range(nq // TILE):
             block(qb)
-            if qb == 2:
+            if qb == 1:
                 @pl.when(h < last - 1)
                 def _():
                     gather_forward(h + 2)
-
-                @pl.when(h < last - 2)
-                def _():
-                    gather_start(h + 3)
 
         top = jnp.max(block_max[slot], axis=0, keepdims=True)
         share = jnp.exp(block_max[slot] - top)
@@ -285,8 +295,8 @@
     def second_pass(h, final):
         slot = h % SLOTS
         gain = gain_ref[h]
-        qx[:, :LANES] = qd[h]
-        ket[:64, :] = jnp.transpose(kv[h].astype(F32))[:64].astype(BF16)
+        qx[:, :LANES] = of_queries(h)
+        ket[:64, :] = jnp.transpose(of_keys(h).astype(F32))[:64].astype(BF16)
         bytes_of(stats.at[h, pl.ds(0, nz - 1)], st_recv.at[h])
         top = stats[h, 0, 0:8, :]
         for other in range(1, nz):
@@ -348,7 +358,7 @@
                 here = slice(at, at + TILE)
                 col_t = jnp.transpose(col_emb[here, :])
                 emb_out[1, :, here] = (-2.0 * (
-                    col_t[ONE_LANE:ONE_LANE + 1, :] * ek[:, here].astype(F32) - col_t[:64, :]
+                    col_t[ONE_LANE:ONE_LANE + 1, :] * ket[64:128, here].astype(F32) - col_t[:64, :]
                 )).astype(BF16)
                 for part in range(TILE // rows):
                     other = kb * (TILE // rows) + part
@@ -377,8 +387,6 @@
             second_pass(t - 2, False)
         return 0
 
-    gather_end(0)
-    gather_forward(1)
     lax.fori_loop(0, heads + 1, step, 0)
     second_pass(last, True)
     emb_in[0, z] = emb_out[0, :, pl.ds(own_q, rows)]
@@ -398,24 +406,19 @@
         dv_ref[:, cols] = jnp.concatenate([kv0[:, 64:], kv1[:, 64:]], axis=1).astype(BF16)
 
     def gather_sent(msg):
-        whole_q, whole_k = (eq, ek) if msg is None else (qd.at[msg], kv.at[msg])
-        if msg is None:
-            whole_q, whole_k = eq.at[:, pl.ds(0, nq - rows)], ek.at[:, pl.ds(0, nk - rows)]
-        else:
-            whole_q = qd.at[msg, pl.ds(0, nq - rows), :]
-            whole_k = kv.at[msg, pl.ds(0, nk - rows), :]
-        bytes_of(whole_q, gz_send.at[number(msg)])
-        bytes_of(whole_k, ga_send.at[number(msg)])
+        first, size = (64 + msg * rows, rows) if msg else (0, 64 + rows)
+        bytes_of(qbuf.at[pl.ds(0, nz - 1), pl.ds(first, size), :], gz_send.at[msg])
+        bytes_of(kbuf.at[pl.ds(0, na - 1), pl.ds(first, size), :], ga_send.at[msg])
 
     for pair in range(heads // 2 - 1):
         reduce_pair(pair)
-    gather_sent(None)
     for h in range(heads):
         gather_sent(h)
         bytes_of(stats.at[h, pl.ds(0, nz - 1)], st_send.at[h])
     bytes_of(emb_in.at[1, pl.ds(0, na - 1)], em_recv.at[1])
     bytes_of(emb_in.at[0, pl.ds(0, nz - 1)], em_recv.at[0])
     mine = jnp.sum(emb_in[0].astype(F32), axis=0) + jnp.sum(emb_in[1].astype(F32), axis=0)
+    mine = mine.astype(BF16)
     head_out[...] = mine
     for step in range(1, nh):
         pltpu.make_async_remote_copy(
@@ -430,7 +433,7 @@
     bytes_of(emb_in.at[1, pl.ds(0, na - 1)], em_send.at[1])
     bytes_of(head_in.at[pl.ds(0, nh - 1)], hd_send)
     bytes_of(head_in.at[pl.ds(0, nh - 1)], hd_recv)
-    de_ref[...] = jnp.sum(head_in[...], axis=0)
+    de_ref[...] = jnp.sum(head_in[...].astype(F32), axis=0)
 
 
 def hand_over(*refs):
@@ -461,10 +464,8 @@
             pltpu.VMEM((rows, width), BF16),
             pltpu.VMEM((64, rows), BF16),
             dma((5,)),
-            pltpu.VMEM((heads, nq, LANES), BF16),
-            pltpu.VMEM((heads, nk, LANES), BF16),
-            pltpu.VMEM((64, nq), BF16),
-            pltpu.VMEM((64, nk), BF16),
+            pltpu.VMEM((nz, 64 + heads * rows, LANES), BF16),
+            pltpu.VMEM((na, 64 + heads * rows, LANES), BF16),
             pltpu.VMEM((nk, 2 * LANES), BF16),
             pltpu.VMEM((nq, 2 * LANES), BF16),
             pltpu.VMEM((nq, LANES), BF16),
@@ -491,10 +492,10 @@
             pltpu.VMEM((heads, na, rows, LANES), BF16),
             pltpu.VMEM((2, 64, max(nq, nk)), BF16),
             pltpu.VMEM((2, max(na, nz), 64, rows), BF16),
-            pltpu.VMEM((64, rows), F32),
-            pltpu.VMEM((nh, 64, rows), F32),
-            dma((heads + 1,)), dma((heads + 1, nz)),
-            dma((heads + 1,)), dma((heads + 1, na)),
+            pltpu.VMEM((64, rows), BF16),
+            pltpu.VMEM((nh, 64, rows), BF16),
+            dma((heads,)), dma((heads, nz)),
+            dma((heads,)), dma((heads, na)),
             dma((heads,)), dma((heads,)),
             dma((heads,)), dma((heads,)),
             dma((heads,)), dma((heads,)),

time: 58.5 us -> 56.8 us (0.971)
  Pallas kernels: 57.6 us -> 56 us
    pallas_call x1, Pallas kernels: 56 us -> 54.4 us  [on_device(): pl.pallas_call(functools.partial(kernel, na, nz, nh), out_shape=(jax.Shap...]
where the time goes in v3:
time: 56.8 us; the launch traced here: 56.6 us
  Pallas kernels  56 us (99%)
  between operations  0.64 us (1%)
    pallas_call x1, Pallas kernels, on_device(): pl.pallas_call(functools.partial(kernel, na, nz, nh), out_shape=(jax.Shap...  54.4 us
    pallas_call x1, Pallas kernels, on_device(): pl.pallas_call(hand_over, out_shape=tuple((jax.ShapeDtypeStruct(r.shape,...  1.59 us

profile of v3, /device:TPU:1, one launch (start us, length us, event | category | flops | bytes accessed | tf_op | source)
XLA Modules:
  0.0 56.6 jit_solution(8444649243869759810)
XLA Ops:
  0.6 54.4 %shard_map.93 = (bf16[128,256]{1,0:T(8,128)(2,1)}, bf16[128,256]{1,0:T(8,128)(2,1)}, bf16[128,256]{1,0:T(8,128)(2,1)}, f32[64,128]{1,0:T(8,128)}) custom-call(f32[4]{0:T(128)} %gain_ref.1, bf16[128,256]{1,0:T(8,128)(2,1)} %q_ref.1, bf16[128,256]{1,0:T(8,128)(2,1)} %k_ref.1, bf16[128,256]{1,0:T(8,128)(2,1)} %v_ref.1, bf16[128,256]{1,0:T(8,128)(2,1)} %g_ref.1, ...), custom_call_target="tpu_custom_call" | custom-call | tf_op jit(solution)/shard_map/pallas_call | solution.py:450
  55.1 1.6 %shard_map.94 = (bf16[128,256]{1,0:T(8,128)(2,1)}, bf16[128,256]{1,0:T(8,128)(2,1)}, bf16[128,256]{1,0:T(8,128)(2,1)}, f32[64,128]{1,0:T(8,128)}) custom-call(bf16[128,256]{1,0:T(8,128)(2,1)} %get-tuple-element.12.refs_0_, bf16[128,256]{1,0:T(8,128)(2,1)} %get-tuple-element.13.refs_1_, bf16[128,256]{1,0:T(8,128)(2,1)} %get-tuple-element.14.refs_2_, ...), custom_call_target="tpu_custom_call" | custom-call | tf_op jit(solution)/shard_map/pallas_call | solution.py:510

commit v4 on v3

--- a/solution.py
+++ b/solution.py
@@ -53,7 +53,7 @@
     na, nz, nh,
     gain_ref, q_ref, k_ref, v_ref, g_ref, emb_ref,
     dq_ref, dk_ref, dv_ref, de_ref,
-    q_in, k_in, v_in, g_in, emb_in_place, in_sem,
+    q_in, k_in, v_in, g_in, emb_in_place, in_sem, total_emb, out_sem,
     qbuf, kbuf, ka, qa, gq, qx, ket, eqt, twice_q, tail_q, tail_k,
     scores, probs, wd16, block_max, totals, moments, shares, stats, combined,
     row_emb, col_emb, dq_out, dkv_out, dq_in, dkv_in,
@@ -392,6 +392,13 @@
     emb_in[0, z] = emb_out[0, :, pl.ds(own_q, rows)]
     emb_in[1, a] = emb_out[1, :, pl.ds(own_k, rows)]
 
+    def results_of(pair):
+        cols = pl.ds(pair * LANES, LANES)
+        return [
+            pltpu.make_async_copy(source.at[:, cols], dest.at[:, cols], out_sem.at[pair, i])
+            for i, (source, dest) in enumerate(((q_in, dq_ref), (k_in, dk_ref), (v_in, dv_ref)))
+        ]
+
     def reduce_pair(pair):
         halves = []
         for h in (2 * pair, 2 * pair + 1):
@@ -401,9 +408,11 @@
                 jnp.sum(dq_in[h].astype(F32), axis=0), jnp.sum(dkv_in[h].astype(F32), axis=0)))
         cols = slice(pair * LANES, (pair + 1) * LANES)
         (q0, kv0), (q1, kv1) = halves
-        dq_ref[:, cols] = jnp.transpose(jnp.concatenate([q0, q1], axis=0)).astype(BF16)
-        dk_ref[:, cols] = jnp.concatenate([kv0[:, :64], kv1[:, :64]], axis=1).astype(BF16)
-        dv_ref[:, cols] = jnp.concatenate([kv0[:, 64:], kv1[:, 64:]], axis=1).astype(BF16)
+        q_in[:, cols] = jnp.transpose(jnp.concatenate([q0, q1], axis=0)).astype(BF16)
+        k_in[:, cols] = jnp.concatenate([kv0[:, :64], kv1[:, :64]], axis=1).astype(BF16)
+        v_in[:, cols] = jnp.concatenate([kv0[:, 64:], kv1[:, 64:]], axis=1).astype(BF16)
+        for copy in results_of(pair):
+            copy.start()
 
     def gather_sent(msg):
         first, size = (64 + msg * rows, rows) if msg else (0, 64 + rows)
@@ -426,14 +435,20 @@
             device_id=(seq, (head + step) % nh), device_id_type=MESH).start()
     head_in[head] = mine
     reduce_pair(heads // 2 - 1)
+    bytes_of(head_in.at[pl.ds(0, nh - 1)], hd_recv)
+    total_emb[...] = jnp.sum(head_in[...].astype(F32), axis=0)
+    leaving = pltpu.make_async_copy(total_emb, de_ref, in_sem.at[0])
+    leaving.start()
     for h in range(heads):
         bytes_of(dq_in.at[h, pl.ds(0, nz - 1)], dq_send.at[h])
         bytes_of(dkv_in.at[h, pl.ds(0, na - 1)], dkv_send.at[h])
     bytes_of(emb_in.at[0, pl.ds(0, nz - 1)], em_send.at[0])
     bytes_of(emb_in.at[1, pl.ds(0, na - 1)], em_send.at[1])
     bytes_of(head_in.at[pl.ds(0, nh - 1)], hd_send)
-    bytes_of(head_in.at[pl.ds(0, nh - 1)], hd_recv)
-    de_ref[...] = jnp.sum(head_in[...].astype(F32), axis=0)
+    for pair in range(heads // 2):
+        for copy in results_of(pair):
+            copy.wait()
+    leaving.wait()
 
 
 def hand_over(*refs):
@@ -456,7 +471,7 @@
             jax.ShapeDtypeStruct((64, rows), F32),
         ),
         in_specs=[pl.BlockSpec(memory_space=pltpu.SMEM)] + [pl.BlockSpec(memory_space=pl.ANY)] * 5,
-        out_specs=(vmem,) * 4,
+        out_specs=(pl.BlockSpec(memory_space=pl.ANY),) * 4,
         scratch_shapes=[
             pltpu.VMEM((rows, width), BF16),
             pltpu.VMEM((rows, width), BF16),
@@ -464,6 +479,8 @@
             pltpu.VMEM((rows, width), BF16),
             pltpu.VMEM((64, rows), BF16),
             dma((5,)),
+            pltpu.VMEM((64, rows), F32),
+            dma((width // LANES, 3)),
             pltpu.VMEM((nz, 64 + heads * rows, LANES), BF16),
             pltpu.VMEM((na, 64 + heads * rows, LANES), BF16),
             pltpu.VMEM((nk, 2 * LANES), BF16),

time: 56.8 us -> 56.8 us (level)
  no operation moved by 1% of the time
where the time goes in v4:
time: 56.8 us; the launch traced here: 56.6 us
  Pallas kernels  56 us (99%)
  between operations  0.64 us (1%)
    pallas_call x1, Pallas kernels, on_device(): pl.pallas_call(functools.partial(kernel, na, nz, nh), out_shape=(jax.Shap...  54.4 us
    pallas_call x1, Pallas kernels, on_device(): pl.pallas_call(hand_over, out_shape=tuple((jax.ShapeDtypeStruct(r.shape,...  1.59 us

profile of v4, /device:TPU:1, one launch (start us, length us, event | category | flops | bytes accessed | tf_op | source)
XLA Modules:
  0.0 56.6 jit_solution(5668834063132894651)
XLA Ops:
  0.6 54.4 %shard_map.93 = (bf16[128,256]{1,0:T(8,128)(2,1)}, bf16[128,256]{1,0:T(8,128)(2,1)}, bf16[128,256]{1,0:T(8,128)(2,1)}, f32[64,128]{1,0:T(8,128)}) custom-call(f32[4]{0:T(128)} %gain_ref.1, bf16[128,256]{1,0:T(8,128)(2,1)} %q_ref.1, bf16[128,256]{1,0:T(8,128)(2,1)} %k_ref.1, bf16[128,256]{1,0:T(8,128)(2,1)} %v_ref.1, bf16[128,256]{1,0:T(8,128)(2,1)} %g_ref.1, ...), custom_call_target="tpu_custom_call" | custom-call | tf_op jit(solution)/shard_map/pallas_call | solution.py:465
  55.0 1.6 %shard_map.94 = (bf16[128,256]{1,0:T(8,128)(2,1)}, bf16[128,256]{1,0:T(8,128)(2,1)}, bf16[128,256]{1,0:T(8,128)(2,1)}, f32[64,128]{1,0:T(8,128)}) custom-call(bf16[128,256]{1,0:T(8,128)(2,1)} %get-tuple-element.12.refs_0_, bf16[128,256]{1,0:T(8,128)(2,1)} %get-tuple-element.13.refs_1_, bf16[128,256]{1,0:T(8,128)(2,1)} %get-tuple-element.14.refs_2_, ...), custom_call_target="tpu_custom_call" | custom-call | tf_op jit(solution)/shard_map/pallas_call | solution.py:527

commit v5 on v4

--- a/solution.py
+++ b/solution.py
@@ -81,18 +81,6 @@
     def a_device(place):
         return (place * nz + z, head)
 
-    barrier = pltpu.get_barrier_semaphore()
-
-    def greet(target):
-        pl.semaphore_signal(barrier, inc=1, device_id=target, device_id_type=MESH)
-
-    for step in range(1, nz):
-        greet(z_device(z_at(step)))
-    for step in range(1, na):
-        greet(a_device((a + step) % na))
-    for step in range(1, nh):
-        greet((seq, (head + step) % nh))
-
     loads = [
         pltpu.make_async_copy(source, dest, in_sem.at[i])
         for i, (source, dest) in enumerate((
@@ -100,6 +88,18 @@
     ]
     for load in loads:
         load.start()
+
+    barrier = pltpu.get_barrier_semaphore()
+
+    def greet(target):
+        pl.semaphore_signal(barrier, inc=1, device_id=target, device_id_type=MESH)
+
+    for step in range(1, nz):
+        greet(z_device(z_at(step)))
+    for step in range(1, na):
+        greet(a_device((a + step) % na))
+    for step in range(1, nh):
+        greet((seq, (head + step) % nh))
 
     def head_rows(h):
         return pl.ds(pl.multiple_of(64 + h * rows, 64), rows)

time: 56.8 us -> 56.8 us (level)
  no operation moved by 1% of the time
where the time goes in v5:
time: 56.8 us; the launch traced here: 56.6 us
  Pallas kernels  56 us (99%)
  between operations  0.64 us (1%)
    pallas_call x1, Pallas kernels, on_device(): pl.pallas_call(functools.partial(kernel, na, nz, nh), out_shape=(jax.Shap...  54.4 us
    pallas_call x1, Pallas kernels, on_device(): pl.pallas_call(hand_over, out_shape=tuple((jax.ShapeDtypeStruct(r.shape,...  1.59 us

profile of v5, /device:TPU:1, one launch (start us, length us, event | category | flops | bytes accessed | tf_op | source)
XLA Modules:
  0.0 56.6 jit_solution(6795921880089973901)
XLA Ops:
  0.6 54.4 %shard_map.93 = (bf16[128,256]{1,0:T(8,128)(2,1)}, bf16[128,256]{1,0:T(8,128)(2,1)}, bf16[128,256]{1,0:T(8,128)(2,1)}, f32[64,128]{1,0:T(8,128)}) custom-call(f32[4]{0:T(128)} %gain_ref.1, bf16[128,256]{1,0:T(8,128)(2,1)} %q_ref.1, bf16[128,256]{1,0:T(8,128)(2,1)} %k_ref.1, bf16[128,256]{1,0:T(8,128)(2,1)} %v_ref.1, bf16[128,256]{1,0:T(8,128)(2,1)} %g_ref.1, ...), custom_call_target="tpu_custom_call" | custom-call | tf_op jit(solution)/shard_map/pallas_call | solution.py:465
  55.0 1.6 %shard_map.94 = (bf16[128,256]{1,0:T(8,128)(2,1)}, bf16[128,256]{1,0:T(8,128)(2,1)}, bf16[128,256]{1,0:T(8,128)(2,1)}, f32[64,128]{1,0:T(8,128)}) custom-call(bf16[128,256]{1,0:T(8,128)(2,1)} %get-tuple-element.12.refs_0_, bf16[128,256]{1,0:T(8,128)(2,1)} %get-tuple-element.13.refs_1_, bf16[128,256]{1,0:T(8,128)(2,1)} %get-tuple-element.14.refs_2_, ...), custom_call_target="tpu_custom_call" | custom-call | tf_op jit(solution)/shard_map/pallas_call | solution.py:527
